TPU v7x, 32 devices: a whole 2x2x4 slice. The times are simulated.
32 devices in a mesh: dp: 16 (over z, y, core), seq: 2 (over x).
Axes of the slice: x: 2, y: 2, z: 4, core: 2. Of those that a mesh axis runs over, the one named last changes fastest.
Arguments:
- tokens: bfloat16 [16, 1024, 1024], P('dp', 'seq'), may hold values from -6 to 6
- cotangent: bfloat16 [16, 1024, 1024], P('dp', 'seq'), may hold values from -6 to 6
- attend_in: float32 [1024, 4096], P(('dp', 'seq')), may hold values from -0.1875 to 0.1875
- attend_in_first: float32 [1024, 4096], P(('dp', 'seq')), may hold values from -40 to 40
- attend_in_second: float32 [1024, 4096], P(('dp', 'seq')), may hold values from 32.768 to 131.072
- attend_out: float32 [2048, 1024], P(('dp', 'seq')), may hold values from -0.5 to 0.5
- attend_out_first: float32 [2048, 1024], P(('dp', 'seq')), may hold values from -40 to 40
- attend_out_second: float32 [2048, 1024], P(('dp', 'seq')), may hold values from 40.96 to 163.84
- gate_up: float32 [1024, 6144], P(('dp', 'seq')), may hold values from -0.1875 to 0.1875
- gate_up_first: float32 [1024, 6144], P(('dp', 'seq')), may hold values from -40 to 40
- gate_up_second: float32 [1024, 6144], P(('dp', 'seq')), may hold values from 16.384 to 65.536
- down_weight: float32 [3072, 1024], P(('dp', 'seq')), may hold values from -0.109375 to 0.109375
- down_first: float32 [3072, 1024], P(('dp', 'seq')), may hold values from -40 to 40
- down_second: float32 [3072, 1024], P(('dp', 'seq')), may hold values from 40.96 to 163.84
- norm_gains: float32 [2, 1024], P(None, ('dp', 'seq')), may hold values from 0.5 to 1.5
- norm_first: float32 [2, 1024], P(None, ('dp', 'seq')), may hold values from -192 to 192
- norm_second: float32 [2, 1024], P(None, ('dp', 'seq')), may hold values from 491.52 to 1966.08
- head_gains: float32 [256], P(('dp', 'seq')), may hold values from 0.5 to 1.5
- head_first: float32 [256], P(('dp', 'seq')), may hold values from -192 to 192
- head_second: float32 [256], P(('dp', 'seq')), may hold values from 491.52 to 1966.08
Outputs:
- activations: bfloat16 [16, 1024, 1024], P('dp', 'seq')
- input_grad: float32 [16, 1024, 1024], P('dp', 'seq')
- attend_in_grad: float32 [1024, 4096], P(('dp', 'seq'))
- attend_in_next: float32 [1024, 4096], P(('dp', 'seq'))
- attend_in_first_next: float32 [1024, 4096], P(('dp', 'seq'))
- attend_in_second_next: float32 [1024, 4096], P(('dp', 'seq'))
- attend_out_grad: float32 [2048, 1024], P(('dp', 'seq'))
- attend_out_next: float32 [2048, 1024], P(('dp', 'seq'))
- attend_out_first_next: float32 [2048, 1024], P(('dp', 'seq'))
- attend_out_second_next: float32 [2048, 1024], P(('dp', 'seq'))
- gate_up_grad: float32 [1024, 6144], P(('dp', 'seq'))
- gate_up_next: float32 [1024, 6144], P(('dp', 'seq'))
- gate_up_first_next: float32 [1024, 6144], P(('dp', 'seq'))
- gate_up_second_next: float32 [1024, 6144], P(('dp', 'seq'))
- down_grad: float32 [3072, 1024], P(('dp', 'seq'))
- down_next: float32 [3072, 1024], P(('dp', 'seq'))
- down_first_next: float32 [3072, 1024], P(('dp', 'seq'))
- down_second_next: float32 [3072, 1024], P(('dp', 'seq'))
- norm_grad: float32 [2, 1024], P(None, ('dp', 'seq'))
- norm_step: float32 [2, 1024], P(None, ('dp', 'seq'))
- norm_first_next: float32 [2, 1024], P(None, ('dp', 'seq'))
- norm_second_next: float32 [2, 1024], P(None, ('dp', 'seq'))
- head_grad: float32 [256], P(('dp', 'seq'))
- head_step: float32 [256], P(('dp', 'seq'))
- head_first_next: float32 [256], P(('dp', 'seq'))
- head_second_next: float32 [256], P(('dp', 'seq'))
All inputs are finite; a program needn't handle non-finite values.
Results may differ from a plain program's by a relative error of at most 0.014.
The roundings to bfloat16 on the way count: a program that leaves them out, or rounds other values in their place, can miss the bound.
Values may be sent and summed in bfloat16 or wider, within the bound.
A program may use at most 320 MiB of HBM per device.

v0:
```python
import jax
import jax.numpy as jnp
from jax import lax
from jax.sharding import PartitionSpec as P

QUERY_HEADS = 16
KEY_VALUE_HEADS = 8
HEAD_WIDTH = 128
FF = 3072


norm_eps = 1e-06
rope_base = 1000000.0
neg_fill = -1e30
beta_one = 0.9
beta_two = 0.99
learn_rate = 0.02
weight_decay = 0.1
adam_eps = 1e-08


def rope_tables(positions, head_dim):
    half_dim = head_dim // 2
    freq_index = jnp.arange(half_dim, dtype=jnp.float32)
    inverse_freq = rope_base ** (-2.0 * freq_index / head_dim)
    angles = positions.astype(jnp.float32)[:, None] * inverse_freq[None, :]
    cosine = jnp.concatenate([jnp.cos(angles), jnp.cos(angles)], -1)[:, None, :]
    sine_table = jnp.concatenate([jnp.sin(angles), jnp.sin(angles)], -1)[:, None, :]
    return (cosine, sine_table)


def head_norm(values, gain):
    inverse = lax.rsqrt(jnp.mean(values * values, -1, keepdims=True) + norm_eps)
    unit_values = values * inverse
    return (unit_values * gain, unit_values, inverse)


def rotate_forward(values, cosine, sine_table):
    half_dim = values.shape[-1] // 2
    turned = jnp.concatenate([-values[..., half_dim:], values[..., :half_dim]], -1)
    return values * cosine + turned * sine_table


def rotate_back(gradient, cosine, sine_table):
    half_dim = gradient.shape[-1] // 2
    scaled = gradient * sine_table
    return gradient * cosine + jnp.concatenate(
        [scaled[..., half_dim:], -scaled[..., :half_dim]], -1
    )


def norm_back(gradient, unit_values, inverse, gain):
    weighted = gradient * gain
    return inverse * (weighted - unit_values * jnp.mean(weighted * unit_values, -1, keepdims=True))


def masked_scores(query_rows, keys_gathered_full, offset):
    scale = query_rows.shape[-1] ** (-0.5)
    scores = (
        jnp.einsum(
            "ckgd,lkd->kgcl", query_rows, keys_gathered_full, preferred_element_type=jnp.float32
        )
        * scale
    )
    query_pos = offset + jnp.arange(query_rows.shape[0])
    allowed = jnp.arange(keys_gathered_full.shape[0])[None, :] <= query_pos[:, None]
    return jnp.where(allowed, scores, neg_fill)


def adam_step(master, first_moment, second_moment, gradient):
    first_next = beta_one * first_moment + (1.0 - beta_one) * gradient
    second_next = beta_two * second_moment + (1.0 - beta_two) * gradient * gradient
    stride = first_next / (jnp.sqrt(second_next) + adam_eps) + weight_decay * master
    return (master - learn_rate * stride, first_next, second_next)


def gain_step(first_moment, second_moment, gradient):
    first_next = beta_one * first_moment + (1.0 - beta_one) * gradient
    second_next = beta_two * second_moment + (1.0 - beta_two) * gradient * gradient
    return (first_next / (jnp.sqrt(second_next) + adam_eps), first_next, second_next)


def body(
    tokens,
    cotangent,
    attend_in,
    attend_in_first,
    attend_in_second,
    attend_out,
    attend_out_first,
    attend_out_second,
    gate_up,
    gate_up_first,
    gate_up_second,
    down_weight,
    down_first,
    down_second,
    norm_gains,
    norm_first,
    norm_second,
    head_gains,
    head_first,
    head_second,
):
    narrow_dtype = jnp.bfloat16
    sequence_count, window_length, width = tokens.shape
    token_rows = sequence_count * window_length
    heads_per_group = QUERY_HEADS // KEY_VALUE_HEADS
    query_columns = QUERY_HEADS * HEAD_WIDTH
    key_columns = KEY_VALUE_HEADS * HEAD_WIDTH
    sequence_length = window_length * lax.axis_size("seq")
    in_low = attend_in.astype(narrow_dtype)
    out_low = attend_out.astype(narrow_dtype)
    gate_low = gate_up.astype(narrow_dtype)
    down_low = down_weight.astype(narrow_dtype)
    gathered = (
        lax.all_gather(in_low, ("dp", "seq"), axis=0, tiled=True),
        lax.all_gather(out_low, ("dp", "seq"), axis=0, tiled=True),
        lax.all_gather(gate_low, ("dp", "seq"), axis=0, tiled=True),
        lax.all_gather(down_low, ("dp", "seq"), axis=0, tiled=True),
        lax.all_gather(norm_gains.astype(narrow_dtype), ("dp", "seq"), axis=1, tiled=True),
        lax.all_gather(head_gains.astype(narrow_dtype), ("dp", "seq"), axis=0, tiled=True),
    )
    in_full, out_full, gate_full, down_full, norm_full, head_full = gathered
    norm_vals = norm_full.astype(jnp.float32)
    head_vals = head_full.astype(jnp.float32)
    flat_in = tokens.reshape(token_rows, width).astype(jnp.float32)
    inverse_one = lax.rsqrt(jnp.mean(flat_in * flat_in, -1, keepdims=True) + norm_eps)
    unit_one = flat_in * inverse_one
    normed_one = (unit_one * norm_vals[0]).astype(narrow_dtype)
    joined_heads = jnp.dot(normed_one, in_full, preferred_element_type=jnp.float32)
    query_raw = joined_heads[:, :query_columns].reshape(token_rows, QUERY_HEADS, HEAD_WIDTH)
    key_unnormed = joined_heads[:, query_columns : query_columns + key_columns].reshape(
        token_rows, KEY_VALUE_HEADS, HEAD_WIDTH
    )
    value_low = joined_heads[:, query_columns + key_columns :].astype(narrow_dtype)
    offset = lax.axis_index("seq") * window_length
    positions = jnp.tile(offset + jnp.arange(window_length), sequence_count)
    cosine, sine_table = rope_tables(positions, HEAD_WIDTH)
    query_normed, query_unit, query_inverse = head_norm(query_raw, head_vals[:HEAD_WIDTH])
    key_normed, key_unit, key_inverse = head_norm(key_unnormed, head_vals[HEAD_WIDTH:])
    query_narrowed = rotate_forward(query_normed, cosine, sine_table).astype(narrow_dtype)
    key_low = rotate_forward(key_normed, cosine, sine_table).astype(narrow_dtype)
    keys_gathered_full, values_gathered_full = (
        lax.all_gather(
            key_low.reshape(sequence_count, window_length, key_columns), "seq", axis=1, tiled=True
        ),
        lax.all_gather(
            value_low.reshape(sequence_count, window_length, key_columns), "seq", axis=1, tiled=True
        ),
    )
    keys_gathered_full = keys_gathered_full.reshape(
        sequence_count, sequence_length, KEY_VALUE_HEADS, HEAD_WIDTH
    )
    values_gathered_full = values_gathered_full.reshape(
        sequence_count, sequence_length, KEY_VALUE_HEADS, HEAD_WIDTH
    )
    query_head_groups = query_narrowed.reshape(
        sequence_count, window_length, KEY_VALUE_HEADS, heads_per_group, HEAD_WIDTH
    )

    def attend_forward(block):
        query_rows, keys_seq, values_seq = block
        scores = masked_scores(query_rows, keys_seq, offset)
        top_score = jnp.max(scores, -1, keepdims=True)
        expo = jnp.exp(scores - top_score)
        total = jnp.sum(expo, -1, keepdims=True)
        probs = expo / total
        mixed = jnp.einsum(
            "kgcl,lkd->ckgd",
            probs.astype(narrow_dtype),
            values_seq,
            preferred_element_type=jnp.float32,
        )
        return (mixed, top_score + jnp.log(total))

    mixed, log_totals = lax.map(
        attend_forward, (query_head_groups, keys_gathered_full, values_gathered_full)
    )
    attn_low = mixed.reshape(token_rows, query_columns).astype(narrow_dtype)
    middle = flat_in + jnp.dot(attn_low, out_full, preferred_element_type=jnp.float32)
    inverse_two = lax.rsqrt(jnp.mean(middle * middle, -1, keepdims=True) + norm_eps)
    unit_two = middle * inverse_two
    normed_two = (unit_two * norm_vals[1]).astype(narrow_dtype)
    gate_values = jnp.dot(normed_two, gate_full, preferred_element_type=jnp.float32)
    gate_part = gate_values[:, :FF]
    up_part = gate_values[:, FF:]
    sigma_gate = jax.nn.sigmoid(gate_part)
    silu_gate = gate_part * sigma_gate
    hidden_low = (silu_gate * up_part).astype(narrow_dtype)
    result = middle + jnp.dot(hidden_low, down_full, preferred_element_type=jnp.float32)
    activations = result.astype(narrow_dtype).reshape(tokens.shape)
    refetched = (
        lax.all_gather(in_low, ("dp", "seq"), axis=0, tiled=True),
        lax.all_gather(out_low, ("dp", "seq"), axis=0, tiled=True),
        lax.all_gather(gate_low, ("dp", "seq"), axis=0, tiled=True),
        lax.all_gather(down_low, ("dp", "seq"), axis=0, tiled=True),
    )
    in_back, out_back, gate_back, down_back = refetched
    grad_rows = cotangent.reshape(token_rows, width)
    grad_float = grad_rows.astype(jnp.float32)
    down_grad_local = jnp.einsum(
        "tf,td->fd", hidden_low, grad_rows, preferred_element_type=jnp.float32
    )
    hidden_grad = jnp.einsum("td,fd->tf", grad_rows, down_back, preferred_element_type=jnp.float32)
    gate_grad_part = hidden_grad * up_part * sigma_gate * (1.0 + gate_part * (1.0 - sigma_gate))
    up_grad_part = hidden_grad * silu_gate
    joined_grad = jnp.concatenate([gate_grad_part, up_grad_part], -1).astype(narrow_dtype)
    gate_grad_local = jnp.einsum(
        "td,tf->df", normed_two, joined_grad, preferred_element_type=jnp.float32
    )
    normed_two_grad = jnp.einsum(
        "tf,df->td", joined_grad, gate_back, preferred_element_type=jnp.float32
    )
    norm_two_gain = jnp.sum(normed_two_grad * unit_two, 0)
    middle_grad = grad_float + norm_back(normed_two_grad, unit_two, inverse_two, norm_vals[1])
    attn_grad = middle_grad.astype(narrow_dtype)
    out_grad_local = jnp.einsum(
        "tq,td->qd", attn_low, attn_grad, preferred_element_type=jnp.float32
    )
    narrow_gradient = jnp.einsum(
        "td,qd->tq", attn_grad, out_back, preferred_element_type=jnp.float32
    ).astype(narrow_dtype)
    narrow_gradient = narrow_gradient.reshape(
        sequence_count, window_length, KEY_VALUE_HEADS, heads_per_group, HEAD_WIDTH
    )

    def attend_backward(block):
        query_rows, keys_seq, values_seq, grad_mixed, log_total = block
        scale = query_rows.shape[-1] ** (-0.5)
        scores = masked_scores(query_rows, keys_seq, offset)
        probs = jnp.exp(scores - log_total)
        grad_probs = jnp.einsum(
            "ckgd,lkd->kgcl", grad_mixed, values_seq, preferred_element_type=jnp.float32
        )
        grad_scores = (
            probs * (grad_probs - jnp.sum(probs * grad_probs, -1, keepdims=True))
        ).astype(narrow_dtype)
        grad_query = (
            jnp.einsum("kgcl,lkd->ckgd", grad_scores, keys_seq, preferred_element_type=jnp.float32)
            * scale
        )
        grad_key = (
            jnp.einsum(
                "kgcl,ckgd->lkd", grad_scores, query_rows, preferred_element_type=jnp.float32
            )
            * scale
        )
        grad_value = jnp.einsum(
            "kgcl,ckgd->lkd",
            probs.astype(narrow_dtype),
            grad_mixed,
            preferred_element_type=jnp.float32,
        )
        return (grad_query, grad_key, grad_value)

    query_grads, key_terms, value_terms = lax.map(
        attend_backward,
        (query_head_groups, keys_gathered_full, values_gathered_full, narrow_gradient, log_totals),
    )
    key_row_sums, value_sums = (
        lax.psum_scatter(
            key_terms.reshape(sequence_count, sequence_length, key_columns),
            "seq",
            scatter_dimension=1,
            tiled=True,
        ),
        lax.psum_scatter(
            value_terms.reshape(sequence_count, sequence_length, key_columns),
            "seq",
            scatter_dimension=1,
            tiled=True,
        ),
    )
    key_narrowed = (
        key_row_sums.astype(narrow_dtype)
        .astype(jnp.float32)
        .reshape(token_rows, KEY_VALUE_HEADS, HEAD_WIDTH)
    )
    value_rounded = value_sums.astype(narrow_dtype).reshape(token_rows, key_columns)
    query_rounded = (
        query_grads.astype(narrow_dtype)
        .astype(jnp.float32)
        .reshape(token_rows, QUERY_HEADS, HEAD_WIDTH)
    )
    query_normed_grad = rotate_back(query_rounded, cosine, sine_table)
    key_normed_grad = rotate_back(key_narrowed, cosine, sine_table)
    query_gain_grad = jnp.sum(query_normed_grad * query_unit, (0, 1))
    key_gain_grad = jnp.sum(key_normed_grad * key_unit, (0, 1))
    query_raw_grad = norm_back(query_normed_grad, query_unit, query_inverse, head_vals[:HEAD_WIDTH])
    key_raw_grad = norm_back(key_normed_grad, key_unit, key_inverse, head_vals[HEAD_WIDTH:])
    joined_in_grad = jnp.concatenate(
        [
            query_raw_grad.reshape(token_rows, query_columns).astype(narrow_dtype),
            key_raw_grad.reshape(token_rows, key_columns).astype(narrow_dtype),
            value_rounded,
        ],
        -1,
    )
    in_grad_local = jnp.einsum(
        "td,tq->dq", normed_one, joined_in_grad, preferred_element_type=jnp.float32
    )
    normed_one_grad = jnp.einsum(
        "tq,dq->td", joined_in_grad, in_back, preferred_element_type=jnp.float32
    )
    norm_one_gain = jnp.sum(normed_one_grad * unit_one, 0)
    input_grad = middle_grad + norm_back(normed_one_grad, unit_one, inverse_one, norm_vals[0])
    input_grad = input_grad.reshape(tokens.shape)
    norm_grad_local = jnp.stack([norm_one_gain, norm_two_gain])
    head_grad_local = jnp.concatenate([query_gain_grad, key_gain_grad])
    owned = (
        lax.psum_scatter(in_grad_local, ("dp", "seq"), scatter_dimension=0, tiled=True),
        lax.psum_scatter(out_grad_local, ("dp", "seq"), scatter_dimension=0, tiled=True),
        lax.psum_scatter(gate_grad_local, ("dp", "seq"), scatter_dimension=0, tiled=True),
        lax.psum_scatter(down_grad_local, ("dp", "seq"), scatter_dimension=0, tiled=True),
        lax.psum_scatter(norm_grad_local, ("dp", "seq"), scatter_dimension=1, tiled=True),
        lax.psum_scatter(head_grad_local, ("dp", "seq"), scatter_dimension=0, tiled=True),
    )
    in_grad, out_grad, gate_grad, down_grad, norm_grad, head_grad = owned
    in_next, in_first, in_second = adam_step(attend_in, attend_in_first, attend_in_second, in_grad)
    out_next, out_first, out_second = adam_step(
        attend_out, attend_out_first, attend_out_second, out_grad
    )
    gate_next, gate_first, gate_second = adam_step(
        gate_up, gate_up_first, gate_up_second, gate_grad
    )
    down_next, down_first_next, down_second_next = adam_step(
        down_weight, down_first, down_second, down_grad
    )
    norm_step, norm_first_next, norm_second_next = gain_step(norm_first, norm_second, norm_grad)
    head_step, head_first_next, head_second_next = gain_step(head_first, head_second, head_grad)
    return (
        activations,
        input_grad,
        in_grad,
        in_next,
        in_first,
        in_second,
        out_grad,
        out_next,
        out_first,
        out_second,
        gate_grad,
        gate_next,
        gate_first,
        gate_second,
        down_grad,
        down_next,
        down_first_next,
        down_second_next,
        norm_grad,
        norm_step,
        norm_first_next,
        norm_second_next,
        head_grad,
        head_step,
        head_first_next,
        head_second_next,
    )


def solution(mesh):
    in_specs = (
        P("dp", "seq", None),
        P("dp", "seq", None),
        P(("dp", "seq"), None),
        P(("dp", "seq"), None),
        P(("dp", "seq"), None),
        P(("dp", "seq"), None),
        P(("dp", "seq"), None),
        P(("dp", "seq"), None),
        P(("dp", "seq"), None),
        P(("dp", "seq"), None),
        P(("dp", "seq"), None),
        P(("dp", "seq"), None),
        P(("dp", "seq"), None),
        P(("dp", "seq"), None),
        P(None, ("dp", "seq")),
        P(None, ("dp", "seq")),
        P(None, ("dp", "seq")),
        P(("dp", "seq")),
        P(("dp", "seq")),
        P(("dp", "seq")),
    )
    out_specs = (
        P("dp", "seq", None),
        P("dp", "seq", None),
        P(("dp", "seq"), None),
        P(("dp", "seq"), None),
        P(("dp", "seq"), None),
        P(("dp", "seq"), None),
        P(("dp", "seq"), None),
        P(("dp", "seq"), None),
        P(("dp", "seq"), None),
        P(("dp", "seq"), None),
        P(("dp", "seq"), None),
        P(("dp", "seq"), None),
        P(("dp", "seq"), None),
        P(("dp", "seq"), None),
        P(("dp", "seq"), None),
        P(("dp", "seq"), None),
        P(("dp", "seq"), None),
        P(("dp", "seq"), None),
        P(None, ("dp", "seq")),
        P(None, ("dp", "seq")),
        P(None, ("dp", "seq")),
        P(None, ("dp", "seq")),
        P(("dp", "seq")),
        P(("dp", "seq")),
        P(("dp", "seq")),
        P(("dp", "seq")),
    )
    return jax.shard_map(body, mesh=mesh, in_specs=in_specs, out_specs=out_specs, check_vma=False)
```

profile of v0, /device:TPU:0, one launch (start us, length us, event | category | flops | bytes accessed | tf_op | source)
XLA Modules:
  0.0 1780.6 jit_solution(1874690552712985253)
XLA Ops:
  10.5 69.6 %all-gather.2 = bf16[32,32,2]{1,2,0:T(2,128)(2,1)S(1)} all-gather(bf16[1,32,2]{1,2,0:T(2,128)(2,1)S(1)} %convert_bitcast_fusion.3), channel_id=1, replica_groups=mesh['dp'=16,'seq'=2] {'dp','seq'}, dimensions={0}, use_global_device_ids=true | all-gather | bytes 4224 | tf_op jit(solution)/shard_map/all_gather | solution.py:121
  81.4 36.9 %all-reduce = bf16[256]{0:T(256)(128)(2,1)S(1)} all-reduce(bf16[256]{0:T(256)(128)(2,1)S(1)} %dynamic-update-slice), channel_id=1, replica_groups=mesh['dp'=16,'seq'=2] {'dp','seq'}, use_global_device_ids=true, to_apply=%add | all-reduce | flops 256 | bytes 1024
  118.8 7.1 fusion.62
  141.0 5.1 slice.78
  146.1 5.3 copy.194
  162.4 6.1 all-gather.20.cloned.1.call-done
  175.2 27.9 %all-gather.18.cloned.1.call-done = bf16[1024,1024]{1,0:T(8,128)(2,1)} async-done(((bf16[512,1024]{1,0:T(8,128)(2,1)}), bf16[1024,1024]{1,0:T(8,128)(2,1)}) %all-gather.18.cloned.1.call-update) | async-done | bytes 2097168 | tf_op jit(solution)/shard_map/all_gather | solution.py:148
  206.8 14.0 fusion.9
  220.8 14.4 fusion.3
  235.2 17.0 fusion.44
  252.2 16.5 all-gather.12.cloned.1.call-done
  268.7 6.5 multiply_reduce_fusion.6
  275.2 91.3 %all-gather.14.cloned.1.call-done = bf16[1024,6144]{1,0:T(8,128)(2,1)} async-done(((bf16[32,6144]{1,0:T(8,128)(2,1)}), bf16[1024,6144]{1,0:T(8,128)(2,1)}) %all-gather.14.cloned.1.call-update) | async-done | bytes 12582928 | tf_op jit(solution)/shard_map/all_gather | solution.py:119
  366.6 14.6 fusion.76
  381.1 56.6 %all-gather.16.cloned.1.call-done = bf16[3072,1024]{1,0:T(8,128)(2,1)} async-done(((bf16[96,1024]{1,0:T(8,128)(2,1)}), bf16[3072,1024]{1,0:T(8,128)(2,1)}) %all-gather.16.cloned.1.call-update) | async-done | bytes 6291472 | tf_op jit(solution)/shard_map/all_gather | solution.py:120
  437.8 12.9 multiply_convert_fusion.1
  450.6 13.9 multiply_reduce_fusion.3
  472.2 4.1 copy.204
  476.3 27.6 %fusion = (f32[8,2,512]{2,1,0:T(2,128)S(1)}, f32[8,1024,512,2]{2,1,3,0:T(8,128)}) fusion(f32[8,2,512]{2,1,0:T(2,128)S(1)} %bitcast.267, f32[8,1024,512,2]{2,1,3,0:T(8,128)} %get-tuple-element.122, pred[512,1024]{0,1:T(8,128)(4,1)S(1)} %iota_compare_fusion, bf16[512,8,2,128]{0,3,2,1:T(8,128)(2,1)} %bitcast.246, bf16[1024,8,128,1]{2,1,0,3:T(8,128)(2,1)S(1)} %bitcast.245), kind=kOutput, calls=%fused_computation.2 | convolution fusion | flops 2189418496 | bytes 71892992 | tf_op jit(solution)/shard_map/while/body/eval_jaxpr/ckgd,lkd->kgcl/dot_general | solution.py:233
  503.9 28.7 %fusion.2 = bf16[8,2,512,1024]{2,3,1,0:T(8,128)(2,1)} fusion(f32[8,1024,512,2]{2,1,3,0:T(8,128)} %get-tuple-element.127, f32[8,2,512]{2,1,0:T(2,128)S(1)} %get-tuple-element.126, f32[8,2,512]{2,1,0:T(2,128)S(1)} %bitcast.268, f32[8,1024,512,2]{2,1,3,0:T(8,128)} %get-tuple-element.122, pred[512,1024]{0,1:T(8,128)(4,1)S(1)} %iota_compare_fusion), kind=kLoop, calls=%fused_computation.4 | loop fusion | flops 50331648 | bytes 84475904 | tf_op jit(solution)/shard_map/while/body/eval_jaxpr/convert_element_type | solution.py:238
  532.6 13.2 bitcast_multiply_fusion.3
  545.8 5.3 copy.200
  552.8 17.0 fusion.5
  569.8 5.5 copy.201
  578.6 5.8 copy.173
  584.4 10.3 fusion.40
  594.7 5.5 copy.168
  602.8 4.7 fusion.83
  614.2 6.2 multiply_reduce_fusion
  620.6 5.5 copy.199
  626.2 4.9 pad_maximum_fusion.1
  635.1 10.6 fusion.13
  652.8 8.1 reduce-scatter.12.cloned.1.call-done
  663.5 4.9 fusion.28
  668.5 9.8 fusion.38
  679.4 7.8 fusion.57
  687.8 10.2 fusion.51
  698.7 15.1 fusion.17
  714.1 10.5 fusion.48
  727.3 8.7 fusion.50
  738.7 4.4 fusion.31
  743.2 39.5 %all-reduce.1 = f32[256]{0:T(256)S(1)} all-reduce(f32[256]{0:T(256)S(1)} %pad_maximum_fusion.11), channel_id=11, replica_groups=mesh['dp'=16,'seq'=2] {'dp','seq'}, use_global_device_ids=true, to_apply=%region_23.24.clone | all-reduce | flops 256 | bytes 2048
  783.3 4.2 fusion.37
  787.5 26.3 %reduce-scatter.22.cloned.1.call-done = f32[32,2]{1,0:T(8,128)} async-done(((f32[1024,2]{1,0:T(8,128)}), f32[32,2]{1,0:T(8,128)}) %reduce-scatter.22.cloned.1.call-update) | async-done | bytes 272
  815.1 180.6 %reduce-scatter.16.cloned.1.call-done = f32[64,1024]{1,0:T(8,128)} async-done(((f32[2048,1024]{1,0:T(8,128)}), f32[64,1024]{1,0:T(8,128)}) %reduce-scatter.16.cloned.1.call-update) | async-done | bytes 262160 | tf_op jit(solution)/shard_map/reduce_scatter | solution.py:313
  997.8 162.1 %reduce-scatter.20.cloned.1.call-done = f32[96,1024]{1,0:T(8,128)} async-done(((f32[3072,1024]{1,0:T(8,128)}), f32[96,1024]{1,0:T(8,128)}) %reduce-scatter.20.cloned.1.call-update) | async-done | bytes 393232 | tf_op jit(solution)/shard_map/reduce_scatter | solution.py:315
  1162.3 249.2 %reduce-scatter.18.cloned.1.call-done = f32[32,6144]{1,0:T(8,128)} async-done(((f32[1024,6144]{1,0:T(8,128)}), f32[32,6144]{1,0:T(8,128)}) %reduce-scatter.18.cloned.1.call-update) | async-done | bytes 786448 | tf_op jit(solution)/shard_map/reduce_scatter | solution.py:314
  1414.3 357.1 %reduce-scatter.14.cloned.1.call-done = f32[32,4096]{1,0:T(8,128)} async-done(((f32[1024,4096]{1,0:T(8,128)}), f32[32,4096]{1,0:T(8,128)}) %reduce-scatter.14.cloned.1.call-update) | async-done | bytes 524304 | tf_op jit(solution)/shard_map/reduce_scatter | solution.py:312
  (243 shorter events, 96.4 us)
Async XLA Ops:
  7.2 111.1 %copy-start.15 = (bf16[1,512,1024]{2,1,0:T(8,128)(2,1)S(1)}, bf16[1,512,1024]{2,1,0:T(8,128)(2,1)}, u32[]{:S(2)}) copy-start(bf16[1,512,1024]{2,1,0:T(8,128)(2,1)} %param.20) | copy-start | bytes 3145732
  7.2 111.5 %all-gather.10.cloned.1.call-start = ((), (), s32[]{:S(2)}) async-start(), calls=%async_computation.7 | async-start | bytes 8650752 | tf_op jit(solution)/shard_map/all_gather | solution.py:117
  9.1 159.3 %all-gather.20.cloned.1.call-start = ((), (), s32[]{:S(2)}) async-start(), calls=%async_computation.18 | async-start | bytes 3145728 | tf_op jit(solution)/shard_map/all_gather | solution.py:145
  80.9 77.4 %copy-start.22 = (f32[512,128]{0,1:T(8,128)}, f32[512,128]{0,1:T(8,128)S(1)}, u32[]{:S(2)}) copy-start(f32[512,128]{0,1:T(8,128)S(1)} %get-tuple-element.129) | copy-start | bytes 786436
  81.0 48.7 %copy-start.28 = (f32[512,128]{1,0:T(8,128)}, f32[512,128]{1,0:T(8,128)S(1)}, u32[]{:S(2)}) copy-start(f32[512,128]{1,0:T(8,128)S(1)} %copy.154) | copy-start | bytes 786436
  81.2 49.2 %copy-start.26 = (f32[512,128]{1,0:T(8,128)}, f32[512,128]{1,0:T(8,128)S(1)}, u32[]{:S(2)}) copy-start(f32[512,128]{1,0:T(8,128)S(1)} %copy.153) | copy-start | bytes 786436
  118.6 8.6 copy-start.59
  118.6 39.7 %copy-start.57 = (f32[128]{0:T(128)}, f32[128]{0:T(128)S(1)}, u32[]{:S(2)}) copy-start(f32[128]{0:T(128)S(1)} %get-tuple-element.119) | copy-start | bytes 1540
  118.7 7.2 copy-start.51
  118.7 12.5 copy-start.55
  118.7 7.1 copy-start.44
  118.7 345.9 %copy-start.46 = (f32[1,1024]{1,0:T(1,128)}, f32[1,1024]{1,0:T(1,128)S(1)}, u32[]{:S(2)}) copy-start(f32[1,1024]{1,0:T(1,128)S(1)} %get-tuple-element.115) | copy-start | bytes 12292
  125.9 5.3 copy-start.1
  134.7 68.4 %all-gather.18.cloned.1.call-start = ((), (), s32[]{:S(2)}) async-start(), calls=%async_computation.17 | async-start | bytes 3145728 | tf_op jit(solution)/shard_map/all_gather | solution.py:148
  137.6 131.0 %all-gather.12.cloned.1.call-start = ((), (), s32[]{:S(2)}) async-start(), calls=%async_computation.8 | async-start | bytes 4325376 | tf_op jit(solution)/shard_map/all_gather | solution.py:118
  138.4 228.2 %all-gather.14.cloned.1.call-start = ((), (), s32[]{:S(2)}) async-start(), calls=%async_computation.9 | async-start | bytes 12976128 | tf_op jit(solution)/shard_map/all_gather | solution.py:119
  139.3 298.5 %all-gather.16.cloned.1.call-start = ((), (), s32[]{:S(2)}) async-start(), calls=%async_computation.10 | async-start | bytes 6488064 | tf_op jit(solution)/shard_map/all_gather | solution.py:120
  140.1 505.6 %reduce-scatter.10.cloned.1.call-start = ((), (), s32[]{:S(2)}) async-start(), calls=%async_computation.11 | async-start | bytes 6291456 | tf_op jit(solution)/shard_map/reduce_scatter | solution.py:262
  175.2 45.6 %copy-start.8 = (bf16[1024,8,128,1]{0,2,3,1:T(8,128)(2,1)}, bf16[1024,8,128,1]{0,2,3,1:T(8,128)(2,1)S(1)}, u32[]{:S(2)}) copy-start(bf16[1024,8,128,1]{0,2,3,1:T(8,128)(2,1)S(1)} %copy.184) | copy-start | bytes 6291460
  235.2 33.5 %copy-start.16 = (bf16[1,512,1024]{2,1,0:T(8,128)(2,1)S(1)}, bf16[1,512,1024]{2,1,0:T(8,128)(2,1)}, u32[]{:S(2)}) copy-start(bf16[1,512,1024]{2,1,0:T(8,128)(2,1)} %param.20) | copy-start | bytes 3145732
  275.2 189.4 %copy-start.53 = (f32[512]{0:T(512)}, f32[512]{0:T(512)S(1)}, u32[]{:S(2)}) copy-start(f32[512]{0:T(512)S(1)} %add_rsqrt_fusion.2) | copy-start | bytes 6148
  381.1 69.5 %copy-start.21 = (f32[512,1024]{1,0:T(8,128)S(1)}, f32[512,1024]{1,0:T(8,128)}, u32[]{:S(2)}) copy-start(f32[512,1024]{1,0:T(8,128)} %get-tuple-element.124) | copy-start | bytes 6291460
  503.9 28.7 %copy-start.12 = (bf16[512,8,2,128]{0,3,2,1:T(8,128)(2,1)S(1)}, bf16[512,8,2,128]{0,3,2,1:T(8,128)(2,1)}, u32[]{:S(2)}) copy-start(bf16[512,8,2,128]{0,3,2,1:T(8,128)(2,1)} %fusion.16) | copy-start | bytes 6291460
  551.2 109.7 %reduce-scatter.12.cloned.1.call-start = ((), (), s32[]{:S(2)}) async-start(), calls=%async_computation.12 | async-start | bytes 6291456 | tf_op jit(solution)/shard_map/reduce_scatter | solution.py:268
  575.3 238.4 %reduce-scatter.22.cloned.1.call-start = ((), (), s32[]{:S(2)}) async-start(), calls=%async_computation.19 | async-start | bytes 540672
  578.6 5.8 copy-start.9
  594.7 5.5 copy-start.29
  652.7 10.7 copy-start.3
  652.7 10.7 copy-start.56
  662.8 5.6 copy-start.24
  668.5 9.8 copy-start.25
  679.4 316.4 %reduce-scatter.16.cloned.1.call-start = ((), (), s32[]{:S(2)}) async-start(), calls=%async_computation.14 | async-start | bytes 8650752 | tf_op jit(solution)/shard_map/reduce_scatter | solution.py:313
  687.3 472.7 %reduce-scatter.20.cloned.1.call-start = ((), (), s32[]{:S(2)}) async-start(), calls=%async_computation.16 | async-start | bytes 12976128 | tf_op jit(solution)/shard_map/reduce_scatter | solution.py:315
  698.1 713.4 %reduce-scatter.18.cloned.1.call-start = ((), (), s32[]{:S(2)}) async-start(), calls=%async_computation.15 | async-start | bytes 25952256 | tf_op jit(solution)/shard_map/reduce_scatter | solution.py:314
  713.9 1057.5 %reduce-scatter.14.cloned.1.call-start = ((), (), s32[]{:S(2)}) async-start(), calls=%async_computation.13 | async-start | bytes 17301504 | tf_op jit(solution)/shard_map/reduce_scatter | solution.py:312
  738.7 43.9 %copy-start.64 = (f32[8]{0:T(128)S(1)}, f32[8]{0:T(128)}, u32[]{:S(2)}) copy-start(f32[8]{0:T(128)} %param.39) | copy-start | bytes 100
  738.7 43.9 %copy-start.65 = (f32[8]{0:T(128)S(1)}, f32[8]{0:T(128)}, u32[]{:S(2)}) copy-start(f32[8]{0:T(128)} %param.38) | copy-start | bytes 100
  783.3 31.3 %copy-start.62 = (f32[2,32]{1,0:T(2,128)S(1)}, f32[2,32]{1,0:T(2,128)}, u32[]{:S(2)}) copy-start(f32[2,32]{1,0:T(2,128)} %param.36) | copy-start | bytes 772
  783.3 31.3 %copy-start.63 = (f32[2,32]{1,0:T(2,128)S(1)}, f32[2,32]{1,0:T(2,128)}, u32[]{:S(2)}) copy-start(f32[2,32]{1,0:T(2,128)} %param.35) | copy-start | bytes 772
  783.3 212.5 %copy-start.38 = (f32[64,1024]{1,0:T(8,128)S(1)}, f32[64,1024]{1,0:T(8,128)}, u32[]{:S(2)}) copy-start(f32[64,1024]{1,0:T(8,128)} %param.25) | copy-start | bytes 786436
  783.3 376.7 %copy-start.36 = (f32[96,1024]{1,0:T(8,128)S(1)}, f32[96,1024]{1,0:T(8,128)}, u32[]{:S(2)}) copy-start(f32[96,1024]{1,0:T(8,128)} %param.31) | copy-start | bytes 1179652
  783.3 376.7 %copy-start.48 = (f32[96,1024]{1,0:T(8,128)S(1)}, f32[96,1024]{1,0:T(8,128)}, u32[]{:S(2)}) copy-start(f32[96,1024]{1,0:T(8,128)} %param.33) | copy-start | bytes 1179652
  787.5 624.0 %copy-start.33 = (f32[32,6144]{1,0:T(8,128)S(1)}, f32[32,6144]{1,0:T(8,128)}, u32[]{:S(2)}) copy-start(f32[32,6144]{1,0:T(8,128)} %param.28) | copy-start | bytes 2359300
  787.5 624.0 %copy-start.39 = (f32[32,6144]{1,0:T(8,128)S(1)}, f32[32,6144]{1,0:T(8,128)}, u32[]{:S(2)}) copy-start(f32[32,6144]{1,0:T(8,128)} %param.30) | copy-start | bytes 2359300
  787.5 624.0 %copy-start.40 = (f32[32,6144]{1,0:T(8,128)S(1)}, f32[32,6144]{1,0:T(8,128)}, u32[]{:S(2)}) copy-start(f32[32,6144]{1,0:T(8,128)} %param.29) | copy-start | bytes 2359300
  814.6 599.7 %copy-start.61 = (f32[2,32]{1,0:T(2,128)}, f32[2,32]{1,0:T(2,128)S(1)}, u32[]{:S(2)}) copy-start(f32[2,32]{1,0:T(2,128)S(1)} %copy.203) | copy-start | bytes 772
  1162.3 609.1 %copy-start.34 = (f32[32,4096]{1,0:T(8,128)S(1)}, f32[32,4096]{1,0:T(8,128)}, u32[]{:S(2)}) copy-start(f32[32,4096]{1,0:T(8,128)} %param.22) | copy-start | bytes 1572868
  1162.3 609.1 %copy-start.43 = (f32[32,4096]{1,0:T(8,128)S(1)}, f32[32,4096]{1,0:T(8,128)}, u32[]{:S(2)}) copy-start(f32[32,4096]{1,0:T(8,128)} %param.24) | copy-start | bytes 1572868
  (32 other events, 86.7 us)
Sparse Core Ops, SparseCore 0:
  11.6 80.2 all-gather.9
  134.9 33.5 all-gather.19
  170.0 33.1 all-gather.17
  206.6 62.0 all-gather.11
  272.0 94.5 all-gather.13
  369.9 67.8 all-gather.15
  551.3 52.7 reduce-scatter.9
  606.5 54.3 reduce-scatter.11
  679.5 134.2 reduce-scatter.21
  816.6 179.1 reduce-scatter.15
  1003.4 156.5 reduce-scatter.19
  1166.8 244.5 reduce-scatter.17
  1414.4 356.9 reduce-scatter.13
where the time goes:
time: 1790 us; the launch traced here: 1780 us
  waiting for transfers between devices  1180 us (66%)
  matrix products  220 us (12%)
  blocking collectives  146 us (8%)
  other arithmetic  129 us (7%)
  local copies, waits for them, and re-layouts  87.4 us (5%)
    reduce_scatter x1, waiting for transfers between devices, body(): lax.psum_scatter(in_grad_local, ('dp', 'seq'), scatter_dimension=0, tiled...  357 us
    reduce_scatter x1, waiting for transfers between devices, body(): lax.psum_scatter(gate_grad_local, ('dp', 'seq'), scatter_dimension=0, til...  249 us
    reduce_scatter x1, waiting for transfers between devices, body(): lax.psum_scatter(out_grad_local, ('dp', 'seq'), scatter_dimension=0, tile...  181 us
    reduce_scatter x1, waiting for transfers between devices, body(): lax.psum_scatter(down_grad_local, ('dp', 'seq'), scatter_dimension=0, til...  162 us
    all_gather x1, waiting for transfers between devices, body(): lax.all_gather(gate_low, ('dp', 'seq'), axis=0, tiled=True)  91.3 us
    unnamed x2, blocking collectives  76.4 us
    all_gather x1, blocking collectives, body(): lax.all_gather(norm_gains.astype(narrow_dtype), ('dp', 'seq'), axis=1, ti...  69.6 us
    all_gather x1, waiting for transfers between devices, body(): lax.all_gather(down_low, ('dp', 'seq'), axis=0, tiled=True)  56.6 us
  transfers between devices with their start and end apart: 13, of which 11 were waited for; matrix products, arithmetic and copies ran while one was open for 16% of the time, Pallas kernels for 0%

commit v1 on v0

--- a/solution.py
+++ b/solution.py
@@ -78,6 +78,65 @@
     first_next = beta_one * first_moment + (1.0 - beta_one) * gradient
     second_next = beta_two * second_moment + (1.0 - beta_two) * gradient * gradient
     return (first_next / (jnp.sqrt(second_next) + adam_eps), first_next, second_next)
+
+
+def axis_bits():
+    bits = []
+    for name in ("dp", "seq"):
+        count = lax.axis_size(name).bit_length() - 1
+        bits += [(name, bit) for bit in range(count - 1, -1, -1)]
+    return bits
+
+
+def swap(value, bit):
+    name, place = bit
+    pairs = [(i, i ^ (1 << place)) for i in range(lax.axis_size(name))]
+    return lax.ppermute(value, name, pairs)
+
+
+def own_bit(bit):
+    name, place = bit
+    return (lax.axis_index(name) >> place) & 1
+
+
+def halving_order(y_first):
+    rest = [b for b in axis_bits() if b not in (("dp", 0), ("dp", 1)) and b[0] == "dp"]
+    seq = [b for b in axis_bits() if b[0] == "seq"]
+    near, mid = [("dp", 0)], [("dp", 1)]
+    middle = mid + seq if y_first else seq + mid
+    return near + middle + rest[::-1]
+
+
+def scatter_sum(terms, order, wire):
+    bits = [b for b in axis_bits() if b in order]
+    rows = terms.shape[0] >> len(bits)
+    held = terms.reshape((2,) * len(bits) + (rows,) + terms.shape[1:])
+    left = list(bits)
+    for bit in order:
+        at = left.index(bit)
+        mine = own_bit(bit)
+        keep = lax.dynamic_index_in_dim(held, mine, at, keepdims=False)
+        send = lax.dynamic_index_in_dim(held, 1 - mine, at, keepdims=False).astype(wire)
+        held = keep + swap(send, bit).astype(jnp.float32)
+        left.remove(bit)
+    return held
+
+
+def gather_rows(shard, order, busy):
+    bits = [b for b in axis_bits() if b in order]
+    held = shard
+    have = []
+    for bit in order[::-1]:
+        if bit in busy:
+            held, _ = lax.optimization_barrier((held, busy[bit]))
+        got = swap(held, bit)
+        busy[bit] = got
+        have = [b for b in bits if b in have or b == bit]
+        mine = own_bit(bit) == 0
+        held = jnp.stack(
+            [jnp.where(mine, held, got), jnp.where(mine, got, held)], have.index(bit)
+        )
+    return held.reshape((-1,) + shard.shape[1:])
 
 
 def body(
@@ -113,27 +172,40 @@
     out_low = attend_out.astype(narrow_dtype)
     gate_low = gate_up.astype(narrow_dtype)
     down_low = down_weight.astype(narrow_dtype)
-    gathered = (
-        lax.all_gather(in_low, ("dp", "seq"), axis=0, tiled=True),
-        lax.all_gather(out_low, ("dp", "seq"), axis=0, tiled=True),
-        lax.all_gather(gate_low, ("dp", "seq"), axis=0, tiled=True),
-        lax.all_gather(down_low, ("dp", "seq"), axis=0, tiled=True),
-        lax.all_gather(norm_gains.astype(narrow_dtype), ("dp", "seq"), axis=1, tiled=True),
-        lax.all_gather(head_gains.astype(narrow_dtype), ("dp", "seq"), axis=0, tiled=True),
-    )
-    in_full, out_full, gate_full, down_full, norm_full, head_full = gathered
+    x_first = halving_order(False)
+    y_first = halving_order(True)
+    along_seq = [b for b in x_first if b[0] == "seq"]
+    shards = lax.axis_size("dp") * lax.axis_size("seq")
+    norm_part = norm_gains.shape[1]
+    head_part = head_gains.shape[0]
+    gains = jnp.concatenate([norm_gains[0], norm_gains[1], head_gains]).astype(narrow_dtype)
+    gains = jnp.pad(gains, (0, -gains.shape[0] % 128))[None]
+    gains_full = gather_rows(gains, x_first, {})
+    norm_full = jnp.stack(
+        [
+            gains_full[:, :norm_part].reshape(width),
+            gains_full[:, norm_part : 2 * norm_part].reshape(width),
+        ]
+    )
+    head_full = gains_full[:, 2 * norm_part : 2 * norm_part + head_part].reshape(2 * HEAD_WIDTH)
+    busy = {}
+    in_query = gather_rows(in_low[:, :query_columns], x_first, busy)
+    in_key_value = gather_rows(in_low[:, query_columns:], y_first, busy)
+    out_full = gather_rows(out_low, x_first, busy)
+    gate_first_half = gather_rows(gate_low[:, :FF], y_first, busy)
+    gate_second_half = gather_rows(gate_low[:, FF:], x_first, busy)
+    down_full = gather_rows(down_low, y_first, busy)
     norm_vals = norm_full.astype(jnp.float32)
     head_vals = head_full.astype(jnp.float32)
     flat_in = tokens.reshape(token_rows, width).astype(jnp.float32)
     inverse_one = lax.rsqrt(jnp.mean(flat_in * flat_in, -1, keepdims=True) + norm_eps)
     unit_one = flat_in * inverse_one
     normed_one = (unit_one * norm_vals[0]).astype(narrow_dtype)
-    joined_heads = jnp.dot(normed_one, in_full, preferred_element_type=jnp.float32)
-    query_raw = joined_heads[:, :query_columns].reshape(token_rows, QUERY_HEADS, HEAD_WIDTH)
-    key_unnormed = joined_heads[:, query_columns : query_columns + key_columns].reshape(
-        token_rows, KEY_VALUE_HEADS, HEAD_WIDTH
-    )
-    value_low = joined_heads[:, query_columns + key_columns :].astype(narrow_dtype)
+    query_raw = jnp.dot(normed_one, in_query, preferred_element_type=jnp.float32)
+    query_raw = query_raw.reshape(token_rows, QUERY_HEADS, HEAD_WIDTH)
+    key_value = jnp.dot(normed_one, in_key_value, preferred_element_type=jnp.float32)
+    key_unnormed = key_value[:, :key_columns].reshape(token_rows, KEY_VALUE_HEADS, HEAD_WIDTH)
+    value_low = key_value[:, key_columns:].astype(narrow_dtype)
     offset = lax.axis_index("seq") * window_length
     positions = jnp.tile(offset + jnp.arange(window_length), sequence_count)
     cosine, sine_table = rope_tables(positions, HEAD_WIDTH)
@@ -141,14 +213,12 @@
     key_normed, key_unit, key_inverse = head_norm(key_unnormed, head_vals[HEAD_WIDTH:])
     query_narrowed = rotate_forward(query_normed, cosine, sine_table).astype(narrow_dtype)
     key_low = rotate_forward(key_normed, cosine, sine_table).astype(narrow_dtype)
-    keys_gathered_full, values_gathered_full = (
-        lax.all_gather(
-            key_low.reshape(sequence_count, window_length, key_columns), "seq", axis=1, tiled=True
-        ),
-        lax.all_gather(
-            value_low.reshape(sequence_count, window_length, key_columns), "seq", axis=1, tiled=True
-        ),
-    )
+    both_low = jnp.stack([key_low.reshape(token_rows, key_columns), value_low])
+    both_full = gather_rows(
+        both_low.reshape(1, 2, sequence_count, window_length, key_columns), along_seq, {}
+    )
+    keys_gathered_full = jnp.moveaxis(both_full[:, 0], 0, 1)
+    values_gathered_full = jnp.moveaxis(both_full[:, 1], 0, 1)
     keys_gathered_full = keys_gathered_full.reshape(
         sequence_count, sequence_length, KEY_VALUE_HEADS, HEAD_WIDTH
     )
@@ -182,44 +252,47 @@
     inverse_two = lax.rsqrt(jnp.mean(middle * middle, -1, keepdims=True) + norm_eps)
     unit_two = middle * inverse_two
     normed_two = (unit_two * norm_vals[1]).astype(narrow_dtype)
-    gate_values = jnp.dot(normed_two, gate_full, preferred_element_type=jnp.float32)
-    gate_part = gate_values[:, :FF]
-    up_part = gate_values[:, FF:]
+    gate_part = jnp.dot(normed_two, gate_first_half, preferred_element_type=jnp.float32)
+    up_part = jnp.dot(normed_two, gate_second_half, preferred_element_type=jnp.float32)
     sigma_gate = jax.nn.sigmoid(gate_part)
     silu_gate = gate_part * sigma_gate
     hidden_low = (silu_gate * up_part).astype(narrow_dtype)
     result = middle + jnp.dot(hidden_low, down_full, preferred_element_type=jnp.float32)
     activations = result.astype(narrow_dtype).reshape(tokens.shape)
-    refetched = (
-        lax.all_gather(in_low, ("dp", "seq"), axis=0, tiled=True),
-        lax.all_gather(out_low, ("dp", "seq"), axis=0, tiled=True),
-        lax.all_gather(gate_low, ("dp", "seq"), axis=0, tiled=True),
-        lax.all_gather(down_low, ("dp", "seq"), axis=0, tiled=True),
-    )
-    in_back, out_back, gate_back, down_back = refetched
     grad_rows = cotangent.reshape(token_rows, width)
     grad_float = grad_rows.astype(jnp.float32)
     down_grad_local = jnp.einsum(
         "tf,td->fd", hidden_low, grad_rows, preferred_element_type=jnp.float32
     )
-    hidden_grad = jnp.einsum("td,fd->tf", grad_rows, down_back, preferred_element_type=jnp.float32)
+    hidden_grad = jnp.einsum("td,fd->tf", grad_rows, down_full, preferred_element_type=jnp.float32)
     gate_grad_part = hidden_grad * up_part * sigma_gate * (1.0 + gate_part * (1.0 - sigma_gate))
     up_grad_part = hidden_grad * silu_gate
-    joined_grad = jnp.concatenate([gate_grad_part, up_grad_part], -1).astype(narrow_dtype)
-    gate_grad_local = jnp.einsum(
-        "td,tf->df", normed_two, joined_grad, preferred_element_type=jnp.float32
+    down_grad = scatter_sum(down_grad_local, x_first, narrow_dtype)
+    gate_grad_low = gate_grad_part.astype(narrow_dtype)
+    up_grad_low = up_grad_part.astype(narrow_dtype)
+    gate_grad = jnp.concatenate(
+        [
+            scatter_sum(
+                jnp.einsum("td,tf->df", normed_two, part, preferred_element_type=jnp.float32),
+                order,
+                narrow_dtype,
+            )
+            for part, order in ((gate_grad_low, y_first), (up_grad_low, x_first))
+        ],
+        1,
     )
     normed_two_grad = jnp.einsum(
-        "tf,df->td", joined_grad, gate_back, preferred_element_type=jnp.float32
-    )
+        "tf,df->td", gate_grad_low, gate_first_half, preferred_element_type=jnp.float32
+    ) + jnp.einsum("tf,df->td", up_grad_low, gate_second_half, preferred_element_type=jnp.float32)
     norm_two_gain = jnp.sum(normed_two_grad * unit_two, 0)
     middle_grad = grad_float + norm_back(normed_two_grad, unit_two, inverse_two, norm_vals[1])
     attn_grad = middle_grad.astype(narrow_dtype)
     out_grad_local = jnp.einsum(
         "tq,td->qd", attn_low, attn_grad, preferred_element_type=jnp.float32
     )
+    out_grad = scatter_sum(out_grad_local, y_first, narrow_dtype)
     narrow_gradient = jnp.einsum(
-        "td,qd->tq", attn_grad, out_back, preferred_element_type=jnp.float32
+        "td,qd->tq", attn_grad, out_full, preferred_element_type=jnp.float32
     ).astype(narrow_dtype)
     narrow_gradient = narrow_gradient.reshape(
         sequence_count, window_length, KEY_VALUE_HEADS, heads_per_group, HEAD_WIDTH
@@ -258,20 +331,11 @@
         attend_backward,
         (query_head_groups, keys_gathered_full, values_gathered_full, narrow_gradient, log_totals),
     )
-    key_row_sums, value_sums = (
-        lax.psum_scatter(
-            key_terms.reshape(sequence_count, sequence_length, key_columns),
-            "seq",
-            scatter_dimension=1,
-            tiled=True,
-        ),
-        lax.psum_scatter(
-            value_terms.reshape(sequence_count, sequence_length, key_columns),
-            "seq",
-            scatter_dimension=1,
-            tiled=True,
-        ),
-    )
+    both_terms = jnp.stack([key_terms, value_terms]).reshape(
+        2, sequence_count, -1, window_length, key_columns
+    )
+    both_sums = scatter_sum(jnp.moveaxis(both_terms, 2, 0), along_seq, narrow_dtype)[0]
+    key_row_sums, value_sums = both_sums[0], both_sums[1]
     key_narrowed = (
         key_row_sums.astype(narrow_dtype)
         .astype(jnp.float32)
@@ -289,34 +353,41 @@
     key_gain_grad = jnp.sum(key_normed_grad * key_unit, (0, 1))
     query_raw_grad = norm_back(query_normed_grad, query_unit, query_inverse, head_vals[:HEAD_WIDTH])
     key_raw_grad = norm_back(key_normed_grad, key_unit, key_inverse, head_vals[HEAD_WIDTH:])
-    joined_in_grad = jnp.concatenate(
+    query_in_grad = query_raw_grad.reshape(token_rows, query_columns).astype(narrow_dtype)
+    key_value_in_grad = jnp.concatenate(
+        [key_raw_grad.reshape(token_rows, key_columns).astype(narrow_dtype), value_rounded], -1
+    )
+    in_grad = jnp.concatenate(
         [
-            query_raw_grad.reshape(token_rows, query_columns).astype(narrow_dtype),
-            key_raw_grad.reshape(token_rows, key_columns).astype(narrow_dtype),
-            value_rounded,
+            scatter_sum(
+                jnp.einsum("td,tq->dq", normed_one, part, preferred_element_type=jnp.float32),
+                order,
+                narrow_dtype,
+            )
+            for part, order in ((query_in_grad, x_first), (key_value_in_grad, y_first))
         ],
-        -1,
-    )
-    in_grad_local = jnp.einsum(
-        "td,tq->dq", normed_one, joined_in_grad, preferred_element_type=jnp.float32
+        1,
     )
     normed_one_grad = jnp.einsum(
-        "tq,dq->td", joined_in_grad, in_back, preferred_element_type=jnp.float32
+        "tq,dq->td", query_in_grad, in_query, preferred_element_type=jnp.float32
+    ) + jnp.einsum(
+        "tq,dq->td", key_value_in_grad, in_key_value, preferred_element_type=jnp.float32
     )
     norm_one_gain = jnp.sum(normed_one_grad * unit_one, 0)
     input_grad = middle_grad + norm_back(normed_one_grad, unit_one, inverse_one, norm_vals[0])
     input_grad = input_grad.reshape(tokens.shape)
-    norm_grad_local = jnp.stack([norm_one_gain, norm_two_gain])
-    head_grad_local = jnp.concatenate([query_gain_grad, key_gain_grad])
-    owned = (
-        lax.psum_scatter(in_grad_local, ("dp", "seq"), scatter_dimension=0, tiled=True),
-        lax.psum_scatter(out_grad_local, ("dp", "seq"), scatter_dimension=0, tiled=True),
-        lax.psum_scatter(gate_grad_local, ("dp", "seq"), scatter_dimension=0, tiled=True),
-        lax.psum_scatter(down_grad_local, ("dp", "seq"), scatter_dimension=0, tiled=True),
-        lax.psum_scatter(norm_grad_local, ("dp", "seq"), scatter_dimension=1, tiled=True),
-        lax.psum_scatter(head_grad_local, ("dp", "seq"), scatter_dimension=0, tiled=True),
-    )
-    in_grad, out_grad, gate_grad, down_grad, norm_grad, head_grad = owned
+    gain_terms = jnp.concatenate(
+        [
+            norm_one_gain.reshape(shards, norm_part),
+            norm_two_gain.reshape(shards, norm_part),
+            jnp.concatenate([query_gain_grad, key_gain_grad]).reshape(shards, head_part),
+        ],
+        1,
+    )
+    gain_terms = jnp.pad(gain_terms, ((0, 0), (0, -gain_terms.shape[1] % 128)))
+    gain_sums = scatter_sum(gain_terms, x_first, jnp.float32)[0]
+    norm_grad = gain_sums[: 2 * norm_part].reshape(2, norm_part)
+    head_grad = gain_sums[2 * norm_part : 2 * norm_part + head_part]
     in_next, in_first, in_second = adam_step(attend_in, attend_in_first, attend_in_second, in_grad)
     out_next, out_first, out_second = adam_step(
         attend_out, attend_out_first, attend_out_second, out_grad

time: 1790 us -> 979 us (0.55)
  waiting for transfers between devices: 1180 us -> 418 us
  blocking collectives: 146 us -> 0 us
  starting transfers between devices: 1.7 us -> 67.3 us
  other arithmetic: 129 us -> 168 us
  local copies, waits for them, and re-layouts: 87.4 us -> 121 us
  matrix products: 220 us -> 194 us
    reduce_scatter x6 -> x0, waiting for transfers between devices: 957 us -> none  [the longest x1 357 us: body(): lax.psum_scatter(in_grad_local, ('dp', 'seq'), scatter_dimension=0, tiled...]
    ppermute x0 -> x72, waiting for transfers between devices: none -> 418 us  [swap(): return lax.ppermute(value, name, pairs)]
    all_gather x6 -> x0, waiting for transfers between devices: 198 us -> none  [the longest x1 91.3 us: body(): lax.all_gather(gate_low, ('dp', 'seq'), axis=0, tiled=True)]
    unnamed x2 -> x0, blocking collectives: 76.4 us -> none
    all_gather x1 -> x0, blocking collectives: 69.6 us -> none  [body(): lax.all_gather(norm_gains.astype(narrow_dtype), ('dp', 'seq'), axis=1, ti...]
    ppermute x0 -> x72, starting transfers between devices: none -> 67.3 us  [swap(): return lax.ppermute(value, name, pairs)]
    another operation x1 -> x74, other arithmetic: 0.01 us -> 39.7 us  [the longest x72 38.4 us: gather_rows(): jnp.stack([jnp.where(mine, held, got), jnp.where(mine, got, held)], have....]
    add x1 -> x35, other arithmetic: 0.01 us -> 37 us  [the longest x34 37 us: scatter_sum(): held = keep + swap(send, bit).astype(jnp.float32)]
  transfers between devices with their start and end apart: 13 -> 72, of which waited for: 11 -> 49; matrix products, arithmetic and copies ran while one was open for 16% -> 24% of each run, Pallas kernels for 0% -> 0%
where the time goes in v1:
time: 979 us; the launch traced here: 971 us
  waiting for transfers between devices  418 us (43%)
  matrix products  194 us (20%)
  other arithmetic  168 us (17%)
  local copies, waits for them, and re-layouts  121 us (12%)
  starting transfers between devices  67.3 us (7%)
    ppermute x72, waiting for transfers between devices, swap(): return lax.ppermute(value, name, pairs)  418 us
    ppermute x72, starting transfers between devices, swap(): return lax.ppermute(value, name, pairs)  67.3 us
    another operation x72, other arithmetic, gather_rows(): jnp.stack([jnp.where(mine, held, got), jnp.where(mine, got, held)], have....  38.4 us
    add x34, other arithmetic, scatter_sum(): held = keep + swap(send, bit).astype(jnp.float32)  37 us
    unnamed x244, local copies, waits for them, and re-layouts  33.4 us
    convert_element_type x1, other arithmetic, attend_backward(): grad_scores = (probs * (grad_probs - jnp.sum(probs * grad_probs, -1, keep...  28.4 us
    dot_general x1, matrix products, attend_backward(): jnp.einsum('ckgd,lkd->kgcl', grad_mixed, values_seq, preferred_element_ty...  27.6 us
    another operation x4, local copies, waits for them, and re-layouts, body(): jnp.stack([key_terms, value_terms])  27.6 us
  transfers between devices with their start and end apart: 72, of which 49 were waited for; matrix products, arithmetic and copies ran while one was open for 24% of the time, Pallas kernels for 0%

profile of v1, /device:TPU:0, one launch (start us, length us, event | category | flops | bytes accessed | tf_op | source)
XLA Modules:
  0.0 971.5 jit_solution(14461469191804669428)
XLA Ops:
  44.6 11.0 %collective-permute-done.21 = bf16[32,3072]{1,0:T(8,128)(2,1)S(1)} collective-permute-done((bf16[32,3072]{1,0:T(8,128)(2,1)S(1)}, bf16[32,3072]{1,0:T(8,128)(2,1)S(1)}, u32[]{:S(2)}, u32[]{:S(2)}) %collective-permute-start.21) | collective-permute-done | bytes 196640 | tf_op jit(solution)/shard_map/ppermute | solution.py:94
  58.7 7.9 collective-permute-done.26
  70.2 7.8 collective-permute-done.22
  79.3 13.0 %collective-permute-done.10 = bf16[2,2,2,32,2048]{4,3,2,1,0:T(8,128)(2,1)S(1)} collective-permute-done((bf16[2,2,2,32,2048]{4,3,2,1,0:T(8,128)(2,1)S(1)}, bf16[2,2,2,32,2048]{4,3,2,1,0:T(8,128)(2,1)S(1)}, u32[]{:S(2)}, u32[]{:S(2)}) %collective-permute-start.10) | collective-permute-done | bytes 1048608 | tf_op jit(solution)/shard_map/ppermute | solution.py:94
  94.4 9.7 collective-permute-done.11
  107.1 20.6 %collective-permute-done.12 = bf16[2,2,2,32,2048]{4,3,0,1,2:T(8,128)(2,1)S(1)} collective-permute-done((bf16[2,2,2,32,2048]{4,3,0,1,2:T(8,128)(2,1)S(1)}, bf16[2,2,2,32,2048]{4,3,0,1,2:T(8,128)(2,1)S(1)}, u32[]{:S(2)}, u32[]{:S(2)}) %collective-permute-start.12) | collective-permute-done | bytes 1048608 | tf_op jit(solution)/shard_map/ppermute | solution.py:94
  129.9 7.8 collective-permute-done.18
  143.5 6.7 copy.359
  164.8 11.4 %collective-permute-done.23 = bf16[2,2,32,3072]{3,2,0,1:T(8,128)(2,1)S(1)} collective-permute-done((bf16[2,2,32,3072]{3,2,0,1:T(8,128)(2,1)S(1)}, bf16[2,2,32,3072]{3,2,0,1:T(8,128)(2,1)S(1)}, u32[]{:S(2)}, u32[]{:S(2)}) %collective-permute-start.23) | collective-permute-done | bytes 786464 | tf_op jit(solution)/shard_map/ppermute | solution.py:94
  198.9 9.7 collective-permute-done.24
  212.8 20.8 %collective-permute-done.15 = bf16[1,2,1,512,1024]{4,3,1,2,0:T(8,128)(2,1)S(1)} collective-permute-done((bf16[1,2,1,512,1024]{4,3,1,2,0:T(8,128)(2,1)S(1)}, bf16[1,2,1,512,1024]{4,3,1,2,0:T(8,128)(2,1)S(1)}, u32[]{:S(2)}, u32[]{:S(2)}) %collective-permute-start.15) | collective-permute-done | bytes 2097184 | tf_op jit(solution)/shard_map/ppermute | solution.py:94
  249.4 14.1 %fusion.9 = (f32[8,2,512]{2,1,0:T(2,128)S(1)}, f32[8,1024,512,2]{2,1,3,0:T(8,128)}) fusion(pred[512,1024]{0,1:T(8,128)(4,1)S(1)} %iota_compare_fusion, bf16[1024,8,128,1]{0,2,3,1:T(8,128)(2,1)S(1)} %copy.404, bf16[512,8,2,128]{0,3,2,1:T(8,128)(2,1)S(1)} %bitcast.699), kind=kOutput, calls=%fused_computation.14 | convolution fusion | flops 2172641280 | bytes 38305792 | tf_op jit(solution)/shard_map/while/body/eval_jaxpr/ckgd,lkd->kgcl/dot_general | solution.py:60
  263.4 14.5 %fusion.3 = f32[8,2,512]{2,1,0:T(2,128)S(1)} fusion(f32[8,2,512]{2,1,0:T(2,128)S(1)} %get-tuple-element.260, f32[8,1024,512,2]{2,1,3,0:T(8,128)} %get-tuple-element.261, pred[512,1024]{0,1:T(8,128)(4,1)S(1)} %iota_compare_fusion), kind=kLoop, calls=%fused_computation.9 | loop fusion | flops 33546240 | bytes 34144256 | tf_op jit(solution)/shard_map/while/body/eval_jaxpr/reduce_sum | solution.py:237
  277.9 16.4 %fusion.69 = bf16[8,128,2,512]{3,1,2,0:T(8,128)(2,1)} fusion(f32[8,2,512]{2,1,0:T(2,128)S(1)} %fusion.3, f32[8,2,512]{2,1,0:T(2,128)S(1)} %get-tuple-element.260, f32[8,1024,512,2]{2,1,3,0:T(8,128)} %get-tuple-element.261, pred[512,1024]{0,1:T(8,128)(4,1)S(1)} %iota_compare_fusion, bf16[1024,8,128,1]{2,1,0,3:T(8,128)(2,1)S(1)} %bitcast.702), kind=kOutput, calls=%fused_computation.179 | convolution fusion | flops 2190475264 | bytes 38338560 | tf_op jit(solution)/shard_map/while/body/eval_jaxpr/kgcl,lkd->ckgd/dot_general | solution.py:239
  320.1 10.3 %fusion.10 = (bf16[3072,512]{0,1:T(8,128)(2,1)}, f32[512,3072]{1,0:T(8,128)}) fusion(f32[512,3072]{1,0:T(8,128)} %fusion.167, bf16[512,1024]{1,0:T(8,128)(2,1)S(1)} %multiply_convert_fusion.4, bf16[1024,3072]{1,0:T(8,128)(2,1)S(1)} %bitcast.721), kind=kOutput, calls=%fused_computation.26 | convolution fusion | flops 3230662656 | bytes 23068672 | tf_op jit(solution)/shard_map/dot_general | solution.py:256
  347.6 5.9 collective-permute-done.62
  362.3 35.5 %collective-permute-done.63 = bf16[2,2,2,96,1024]{4,3,2,1,0:T(8,128)(2,1)} collective-permute-done((bf16[2,2,2,96,1024]{4,3,2,1,0:T(8,128)(2,1)S(1)}, bf16[2,2,2,96,1024]{4,3,2,1,0:T(8,128)(2,1)}, u32[]{:S(2)}, u32[]{:S(2)}) %collective-permute-start.63) | collective-permute-done | bytes 1572896 | tf_op jit(solution)/shard_map/ppermute | solution.py:94
  402.9 18.4 %collective-permute-done.64 = bf16[2,2,96,1024]{3,2,1,0:T(8,128)(2,1)S(1)} collective-permute-done((bf16[2,2,96,1024]{3,2,1,0:T(8,128)(2,1)S(1)}, bf16[2,2,96,1024]{3,2,1,0:T(8,128)(2,1)S(1)}, u32[]{:S(2)}, u32[]{:S(2)}) %collective-permute-start.64) | collective-permute-done | bytes 786464 | tf_op jit(solution)/shard_map/ppermute | solution.py:94
  424.2 8.2 collective-permute-done.65
  434.5 7.5 collective-permute-done.66
  444.7 10.3 %collective-permute-done.31 = bf16[96,1024]{1,0:T(8,128)(2,1)S(1)} collective-permute-done((bf16[96,1024]{1,0:T(8,128)(2,1)S(1)}, bf16[96,1024]{1,0:T(8,128)(2,1)S(1)}, u32[]{:S(2)}, u32[]{:S(2)}) %collective-permute-start.31) | collective-permute-done | bytes 196640 | tf_op jit(solution)/shard_map/ppermute | solution.py:94
  455.2 11.0 %collective-permute-done.32 = bf16[2,96,1024]{2,1,0:T(8,128)(2,1)S(1)} collective-permute-done((bf16[2,96,1024]{2,1,0:T(8,128)(2,1)S(1)}, bf16[2,96,1024]{2,1,0:T(8,128)(2,1)S(1)}, u32[]{:S(2)}, u32[]{:S(2)}) %collective-permute-start.32) | collective-permute-done | bytes 393248 | tf_op jit(solution)/shard_map/ppermute | solution.py:94
  467.5 17.5 %collective-permute-done.33 = bf16[2,2,96,1024]{3,2,1,0:T(8,128)(2,1)S(1)} collective-permute-done((bf16[2,2,96,1024]{3,2,1,0:T(8,128)(2,1)S(1)}, bf16[2,2,96,1024]{3,2,1,0:T(8,128)(2,1)S(1)}, u32[]{:S(2)}, u32[]{:S(2)}) %collective-permute-start.33) | collective-permute-done | bytes 786464 | tf_op jit(solution)/shard_map/ppermute | solution.py:94
  485.9 34.0 %collective-permute-done.34 = bf16[2,2,2,96,1024]{4,3,2,1,0:T(8,128)(2,1)S(1)} collective-permute-done((bf16[2,2,2,96,1024]{4,3,2,1,0:T(8,128)(2,1)S(1)}, bf16[2,2,2,96,1024]{4,3,2,1,0:T(8,128)(2,1)S(1)}, u32[]{:S(2)}, u32[]{:S(2)}) %collective-permute-start.34) | collective-permute-done | bytes 1572896 | tf_op jit(solution)/shard_map/ppermute | solution.py:94
  535.1 10.6 %fusion.16 = (bf16[512,3072]{1,0:T(8,128)(2,1)S(1)}, bf16[512,3072]{1,0:T(8,128)(2,1)S(1)}) fusion(f32[512,3072]{1,0:T(8,128)} %get-tuple-element.265, f32[512,3072]{1,0:T(8,128)} %fusion.167, bf16[3072,1024]{1,0:T(8,128)(2,1)} %bitcast.725, bf16[1,512,1024]{2,1,0:T(8,128)(2,1)S(1)} %copy-done.77), kind=kOutput, calls=%fused_computation.38 | convolution fusion | flops 3241672704 | bytes 26214400 | tf_op jit(solution)/shard_map/td,fd->tf/dot_general | solution.py:267
  563.9 27.6 %fusion = (f32[8,2,512]{2,1,0:T(2,128)S(1)}, f32[8,1024,512,2]{2,1,3,0:T(8,128)}) fusion(f32[8,2,512]{2,1,0:T(2,128)S(1)} %bitcast.741, f32[8,1024,512,2]{2,1,3,0:T(8,128)} %get-tuple-element.261, pred[512,1024]{0,1:T(8,128)(4,1)S(1)} %iota_compare_fusion, bf16[512,8,2,128]{0,3,2,1:T(8,128)(2,1)} %bitcast.704, bf16[1024,8,128,1]{2,1,0,3:T(8,128)(2,1)S(1)} %bitcast.703), kind=kOutput, calls=%fused_computation.2 | convolution fusion | flops 2189418496 | bytes 71892992 | tf_op jit(solution)/shard_map/while/body/eval_jaxpr/ckgd,lkd->kgcl/dot_general | solution.py:306
  591.6 16.9 %fusion.38 = f32[1024,8,128]{0,2,1:T(8,128)} fusion(bf16[512,8,2,128]{0,3,2,1:T(8,128)(2,1)} %bitcast.705, f32[8,2,512]{2,1,0:T(2,128)S(1)} %bitcast.742, f32[8,1024,512,2]{2,1,3,0:T(8,128)} %get-tuple-element.261, pred[512,1024]{0,1:T(8,128)(4,1)S(1)} %iota_compare_fusion), kind=kOutput, calls=%fused_computation.105 | convolution fusion | flops 2181038080 | bytes 40402944 | tf_op jit(solution)/shard_map/while/body/eval_jaxpr/kgcl,ckgd->lkd/dot_general | solution.py:322
  608.5 28.4 %fusion.2 = bf16[8,2,512,1024]{2,3,1,0:T(8,128)(2,1)} fusion(f32[8,1024,512,2]{2,1,3,0:T(8,128)} %get-tuple-element.268, f32[8,2,512]{2,1,0:T(2,128)S(1)} %get-tuple-element.267, f32[8,2,512]{2,1,0:T(2,128)S(1)} %bitcast.743, f32[8,1024,512,2]{2,1,3,0:T(8,128)} %get-tuple-element.261, pred[512,1024]{0,1:T(8,128)(4,1)S(1)} %iota_compare_fusion), kind=kLoop, calls=%fused_computation.4 | loop fusion | flops 50331648 | bytes 84475904 | tf_op jit(solution)/shard_map/while/body/eval_jaxpr/convert_element_type | solution.py:311
  637.0 14.0 %fusion.26 = f32[1024,8,128]{0,2,1:T(8,128)} fusion(bf16[512,8,2,128]{0,3,2,1:T(8,128)(2,1)} %bitcast.698, bf16[8,2,512,1024]{2,3,1,0:T(8,128)(2,1)} %fusion.2), kind=kOutput, calls=%fused_computation.62 | convolution fusion | flops 2148532224 | bytes 23068672 | tf_op jit(solution)/shard_map/while/body/eval_jaxpr/kgcl,ckgd->lkd/dot_general | solution.py:317
  651.0 11.2 %bitcast_multiply_fusion.6 = (f32[512,16,128]{0,2,1:T(8,128)}, bf16[8,128,2,512]{3,1,2,0:T(8,128)(2,1)}) fusion(f32[512,128]{0,1:T(8,128)S(1)} %copy-done.45, bf16[1024,8,128,1]{0,2,3,1:T(8,128)(2,1)S(1)} %copy-done.17, bf16[8,2,512,1024]{2,3,1,0:T(8,128)(2,1)} %fusion.2), kind=kOutput, calls=%fused_computation.63 | convolution fusion | flops 2151677952 | bytes 25427968 | tf_op jit(solution)/shard_map/while/body/eval_jaxpr/kgcl,lkd->ckgd/dot_general | solution.py:313
  662.2 6.6 fusion.171
  668.7 6.4 fusion.170
  675.2 6.6 reshape.437
  681.7 7.3 copy.424
  689.0 6.6 reshape.438
  695.6 7.2 copy.425
  737.7 11.0 %fusion.76 = bf16[1,512,1024]{2,1,0:T(8,128)(2,1)} fusion(f32[512,1024]{1,0:T(8,128)S(1)} %copy-done.35, bf16[3072,1024]{1,0:T(8,128)(2,1)} %bitcast.726, f32[512,3072]{1,0:T(8,128)} %get-tuple-element.265, f32[512,3072]{1,0:T(8,128)} %fusion.167), kind=kOutput, calls=%fused_computation.203 | convolution fusion | flops 3231711232 | bytes 22020096 | tf_op jit(solution)/shard_map/dot_general | solution.py:260
  748.7 6.2 collective-permute-done.36
  783.1 7.6 fusion.67
  815.1 15.9 %collective-permute-done.48 = bf16[2,2,2,64,1024]{4,3,2,1,0:T(8,128)(2,1)S(1)} collective-permute-done((bf16[2,2,2,64,1024]{4,3,2,1,0:T(8,128)(2,1)S(1)}, bf16[2,2,2,64,1024]{4,3,2,1,0:T(8,128)(2,1)S(1)}, u32[]{:S(2)}, u32[]{:S(2)}) %collective-permute-start.48) | collective-permute-done | bytes 1048608 | tf_op jit(solution)/shard_map/ppermute | solution.py:94
  841.7 6.3 collective-permute-done.49
  874.1 7.6 collective-permute-done.58
  885.2 10.5 %collective-permute-done.53 = bf16[2,2,2,32,3072]{4,3,0,1,2:T(8,128)(2,1)S(1)} collective-permute-done((bf16[2,2,2,32,3072]{4,3,0,1,2:T(8,128)(2,1)S(1)}, bf16[2,2,2,32,3072]{4,3,0,1,2:T(8,128)(2,1)S(1)}, u32[]{:S(2)}, u32[]{:S(2)}) %collective-permute-start.53) | collective-permute-done | bytes 1572896 | tf_op jit(solution)/shard_map/ppermute | solution.py:94
  897.2 20.9 %collective-permute-done.43 = bf16[2,2,2,32,2048]{4,3,0,1,2:T(8,128)(2,1)S(1)} collective-permute-done((bf16[2,2,2,32,2048]{4,3,0,1,2:T(8,128)(2,1)S(1)}, bf16[2,2,2,32,2048]{4,3,0,1,2:T(8,128)(2,1)S(1)}, u32[]{:S(2)}, u32[]{:S(2)}) %collective-permute-start.43) | collective-permute-done | bytes 1048608 | tf_op jit(solution)/shard_map/ppermute | solution.py:94
  920.5 11.7 %collective-permute-done.59 = bf16[2,2,32,3072]{3,2,0,1:T(8,128)(2,1)S(1)} collective-permute-done((bf16[2,2,32,3072]{3,2,0,1:T(8,128)(2,1)S(1)}, bf16[2,2,32,3072]{3,2,0,1:T(8,128)(2,1)S(1)}, u32[]{:S(2)}, u32[]{:S(2)}) %collective-permute-start.59) | collective-permute-done | bytes 786464 | tf_op jit(solution)/shard_map/ppermute | solution.py:94
  939.1 6.6 collective-permute-done.60
  946.9 6.5 collective-permute-done.55
  959.4 7.5 collective-permute-done.56
  (609 shorter events, 370.2 us)
Async XLA Ops:
  1.9 24.1 %collective-permute-start.5 = (bf16[32,2048]{1,0:T(8,128)(2,1)S(1)}, bf16[32,2048]{1,0:T(8,128)(2,1)S(1)}, u32[]{:S(2)}, u32[]{:S(2)}) collective-permute-start(bf16[32,2048]{1,0:T(8,128)(2,1)S(1)} %slice.143), channel_id=1, source_target_pairs={{0,16},{2,18},{4,20},{6,22},{8,24},{10,26},{12,28},{14,30},{16,0},... | collective-permute-start | bytes 393224 | tf_op jit(solution)/shard_map/ppermute | solution.py:94
  38.7 16.9 %collective-permute-start.8 = (bf16[2,32,2048]{2,1,0:T(8,128)(2,1)S(1)}, bf16[2,32,2048]{2,1,0:T(8,128)(2,1)S(1)}, u32[]{:S(2)}, u32[]{:S(2)}) collective-permute-start(bf16[2,32,2048]{2,1,0:T(8,128)(2,1)S(1)} %pad_maximum_fusion.33), channel_id=1, source_target_pairs={{0,8},{2,10},{4,12},{6,14},{8,0},{10,2},{12,4},{14,6},{16,24},{18,... | collective-permute-start | bytes 786440 | tf_op jit(solution)/shard_map/ppermute | solution.py:94
  40.2 27.9 %collective-permute-start.9 = (bf16[2,2,32,2048]{3,2,1,0:T(8,128)(2,1)S(1)}, bf16[2,2,32,2048]{3,2,1,0:T(8,128)(2,1)S(1)}, u32[]{:S(2)}, u32[]{:S(2)}) collective-permute-start(bf16[2,2,32,2048]{3,2,1,0:T(8,128)(2,1)S(1)} %pad_maximum_fusion.27), channel_id=1, source_target_pairs={{0,4},{2,6},{4,0},{6,2},{8,12},{10,14},{12,8},{14,10},{16,20},{18,... | collective-permute-start | bytes 1572872 | tf_op jit(solution)/shard_map/ppermute | solution.py:94
  55.6 11.1 %collective-permute-start.26 = (bf16[32,3072]{1,0:T(8,128)(2,1)S(1)}, bf16[32,3072]{1,0:T(8,128)(2,1)S(1)}, u32[]{:S(2)}, u32[]{:S(2)}) collective-permute-start(bf16[32,3072]{1,0:T(8,128)(2,1)S(1)} %copy-done.83), channel_id=1, source_target_pairs={{0,16},{2,18},{4,20},{6,22},{8,24},{10,26},{12,28},{14,30},{16,0},... | collective-permute-start | bytes 589832 | tf_op jit(solution)/shard_map/ppermute | solution.py:94
  55.6 12.5 %collective-permute-start.17 = (bf16[2,64,1024]{2,1,0:T(8,128)(2,1)S(1)}, bf16[2,64,1024]{2,1,0:T(8,128)(2,1)S(1)}, u32[]{:S(2)}, u32[]{:S(2)}) collective-permute-start(bf16[2,64,1024]{2,1,0:T(8,128)(2,1)S(1)} %pad_maximum_fusion.37), channel_id=1, source_target_pairs={{0,8},{2,10},{4,12},{6,14},{8,0},{10,2},{12,4},{14,6},{16,24},{18,... | collective-permute-start | bytes 786440 | tf_op jit(solution)/shard_map/ppermute | solution.py:94
  68.3 24.0 %collective-permute-start.10 = (bf16[2,2,2,32,2048]{4,3,2,1,0:T(8,128)(2,1)S(1)}, bf16[2,2,2,32,2048]{4,3,2,1,0:T(8,128)(2,1)S(1)}, u32[]{:S(2)}, u32[]{:S(2)}) collective-permute-start(bf16[2,2,2,32,2048]{4,3,2,1,0:T(8,128)(2,1)S(1)} %pad_maximum_fusion.19), channel_id=1, source_target_pairs={{0,1},{1,0},{2,3},{3,2},{4,5},{5,4},{6,7},{7,6},{8,9},{9,8},{10,11... | collective-permute-start | bytes 3145736 | tf_op jit(solution)/shard_map/ppermute | solution.py:94
  78.0 28.0 %collective-permute-start.27 = (bf16[2,32,3072]{2,1,0:T(8,128)(2,1)S(1)}, bf16[2,32,3072]{2,1,0:T(8,128)(2,1)S(1)}, u32[]{:S(2)}, u32[]{:S(2)}) collective-permute-start(bf16[2,32,3072]{2,1,0:T(8,128)(2,1)S(1)} %pad_maximum_fusion.31), channel_id=1, source_target_pairs={{0,8},{2,10},{4,12},{6,14},{8,0},{10,2},{12,4},{14,6},{16,24},{18,... | collective-permute-start | bytes 1179656 | tf_op jit(solution)/shard_map/ppermute | solution.py:94
  92.3 11.8 %collective-permute-start.11 = (bf16[2,2,32,2048]{3,2,0,1:T(8,128)(2,1)S(1)}, bf16[2,2,32,2048]{3,2,0,1:T(8,128)(2,1)S(1)}, u32[]{:S(2)}, u32[]{:S(2)}) collective-permute-start(bf16[2,2,32,2048]{3,2,0,1:T(8,128)(2,1)S(1)} %pad_maximum_fusion.26), channel_id=1, source_target_pairs={{0,1},{1,0},{2,3},{3,2},{4,5},{5,4},{6,7},{7,6},{8,9},{9,8},{10,11... | collective-permute-start | bytes 1572872 | tf_op jit(solution)/shard_map/ppermute | solution.py:94
  94.3 46.1 %collective-permute-start.13 = (bf16[2,2,2,2,32,2048]{5,4,3,2,1,0:T(8,128)(2,1)S(1)}, bf16[2,2,2,2,32,2048]{5,4,3,2,1,0:T(8,128)(2,1)S(1)}, u32[]{:S(2)}, u32[]{:S(2)}) collective-permute-start(bf16[2,2,2,2,32,2048]{5,4,3,2,1,0:T(8,128)(2,1)S(1)} %pad_maximum_fusion.10), channel_id=1, source_target_pairs={{0,2},{2,0},{4,6},{6,4},{8,10},{10,8},{12,14},{14,12},{16,18},{18,... | collective-permute-start | bytes 6291464 | tf_op jit(solution)/shard_map/ppermute | solution.py:94
  104.3 23.4 %collective-permute-start.12 = (bf16[2,2,2,32,2048]{4,3,0,1,2:T(8,128)(2,1)S(1)}, bf16[2,2,2,32,2048]{4,3,0,1,2:T(8,128)(2,1)S(1)}, u32[]{:S(2)}, u32[]{:S(2)}) collective-permute-start(bf16[2,2,2,32,2048]{4,3,0,1,2:T(8,128)(2,1)S(1)} %pad_maximum_fusion.20), channel_id=1, source_target_pairs={{0,4},{2,6},{4,0},{6,2},{8,12},{10,14},{12,8},{14,10},{16,20},{18,... | collective-permute-start | bytes 3145736 | tf_op jit(solution)/shard_map/ppermute | solution.py:94
  138.8 22.0 %collective-permute-start.19 = (bf16[2,2,2,64,1024]{4,3,2,1,0:T(8,128)(2,1)}, bf16[2,2,2,64,1024]{4,3,2,1,0:T(8,128)(2,1)}, u32[]{:S(2)}, u32[]{:S(2)}) collective-permute-start(bf16[2,2,2,64,1024]{4,3,2,1,0:T(8,128)(2,1)} %pad_maximum_fusion.21), channel_id=1, source_target_pairs={{0,1},{1,0},{2,3},{3,2},{4,5},{5,4},{6,7},{7,6},{8,9},{9,8},{10,11... | collective-permute-start | bytes 3145736 | tf_op jit(solution)/shard_map/ppermute | solution.py:94
  140.5 37.7 %collective-permute-start.14 = (bf16[2,2,2,2,32,2048]{5,4,3,2,1,0:T(8,128)(2,1)S(1)}, bf16[2,2,2,2,32,2048]{5,4,3,2,1,0:T(8,128)(2,1)}, u32[]{:S(2)}, u32[]{:S(2)}) collective-permute-start(bf16[2,2,2,2,32,2048]{5,4,3,2,1,0:T(8,128)(2,1)S(1)} %copy.414), channel_id=1, source_target_pairs={{0,2},{2,0},{4,6},{6,4},{8,10},{10,8},{12,14},{14,12},{16,18},{18,... | collective-permute-start | bytes 6291464 | tf_op jit(solution)/shard_map/ppermute | solution.py:94
  160.8 15.4 %collective-permute-start.23 = (bf16[2,2,32,3072]{3,2,0,1:T(8,128)(2,1)S(1)}, bf16[2,2,32,3072]{3,2,0,1:T(8,128)(2,1)S(1)}, u32[]{:S(2)}, u32[]{:S(2)}) collective-permute-start(bf16[2,2,32,3072]{3,2,0,1:T(8,128)(2,1)S(1)} %copy-done.59), channel_id=1, source_target_pairs={{0,1},{1,0},{2,3},{3,2},{4,5},{5,4},{6,7},{7,6},{8,9},{9,8},{10,11... | collective-permute-start | bytes 2359304 | tf_op jit(solution)/shard_map/ppermute | solution.py:94
  176.4 32.1 %collective-permute-start.24 = (bf16[2,2,2,32,3072]{4,3,0,1,2:T(8,128)(2,1)S(1)}, bf16[2,2,2,32,3072]{4,3,0,1,2:T(8,128)(2,1)S(1)}, u32[]{:S(2)}, u32[]{:S(2)}) collective-permute-start(bf16[2,2,2,32,3072]{4,3,0,1,2:T(8,128)(2,1)S(1)} %pad_maximum_fusion.14), channel_id=1, source_target_pairs={{0,4},{2,6},{4,0},{6,2},{8,12},{10,14},{12,8},{14,10},{16,20},{18,... | collective-permute-start | bytes 4718600 | tf_op jit(solution)/shard_map/ppermute | solution.py:94
  191.3 42.3 %collective-permute-start.15 = (bf16[1,2,1,512,1024]{4,3,1,2,0:T(8,128)(2,1)S(1)}, bf16[1,2,1,512,1024]{4,3,1,2,0:T(8,128)(2,1)S(1)}, u32[]{:S(2)}, u32[]{:S(2)}) collective-permute-start(bf16[1,2,1,512,1024]{4,3,1,2,0:T(8,128)(2,1)S(1)} %maximum_bitcast_fusion.1), channel_id=1, source_target_pairs={{0,1},{1,0},{2,3},{3,2},{4,5},{5,4},{6,7},{7,6},{8,9},{9,8},{10,11... | collective-permute-start | bytes 6291464 | tf_op jit(solution)/shard_map/ppermute | solution.py:94
  198.9 46.7 %collective-permute-start.20 = (bf16[2,2,2,2,64,1024]{5,4,3,2,1,0:T(8,128)(2,1)}, bf16[2,2,2,2,64,1024]{5,4,3,2,1,0:T(8,128)(2,1)}, u32[]{:S(2)}, u32[]{:S(2)}) collective-permute-start(bf16[2,2,2,2,64,1024]{5,4,3,2,1,0:T(8,128)(2,1)} %pad_maximum_fusion.11), channel_id=1, source_target_pairs={{0,2},{2,0},{4,6},{6,4},{8,10},{10,8},{12,14},{14,12},{16,18},{18,... | collective-permute-start | bytes 6291464 | tf_op jit(solution)/shard_map/ppermute | solution.py:94
  211.0 34.6 %collective-permute-start.28 = (bf16[2,2,32,3072]{3,2,1,0:T(8,128)(2,1)S(1)}, bf16[2,2,32,3072]{3,2,1,0:T(8,128)(2,1)}, u32[]{:S(2)}, u32[]{:S(2)}) collective-permute-start(bf16[2,2,32,3072]{3,2,1,0:T(8,128)(2,1)S(1)} %copy-done.58), channel_id=1, source_target_pairs={{0,4},{2,6},{4,0},{6,2},{8,12},{10,14},{12,8},{14,10},{16,20},{18,... | collective-permute-start | bytes 2359304 | tf_op jit(solution)/shard_map/ppermute | solution.py:94
  245.6 55.5 %collective-permute-start.25 = (bf16[2,2,2,2,32,3072]{5,4,3,2,1,0:T(8,128)(2,1)}, bf16[2,2,2,2,32,3072]{5,4,3,2,1,0:T(8,128)(2,1)}, u32[]{:S(2)}, u32[]{:S(2)}) collective-permute-start(bf16[2,2,2,2,32,3072]{5,4,3,2,1,0:T(8,128)(2,1)} %copy.419), channel_id=1, source_target_pairs={{0,2},{2,0},{4,6},{6,4},{8,10},{10,8},{12,14},{14,12},{16,18},{18,... | collective-permute-start | bytes 9437192 | tf_op jit(solution)/shard_map/ppermute | solution.py:94
  248.4 48.8 %collective-permute-start.29 = (bf16[2,2,2,32,3072]{4,3,2,1,0:T(8,128)(2,1)}, bf16[2,2,2,32,3072]{4,3,2,1,0:T(8,128)(2,1)}, u32[]{:S(2)}, u32[]{:S(2)}) collective-permute-start(bf16[2,2,2,32,3072]{4,3,2,1,0:T(8,128)(2,1)} %pad_maximum_fusion.15), channel_id=1, source_target_pairs={{0,1},{1,0},{2,3},{3,2},{4,5},{5,4},{6,7},{7,6},{8,9},{9,8},{10,11... | collective-permute-start | bytes 4718600 | tf_op jit(solution)/shard_map/ppermute | solution.py:94
  301.1 15.3 %collective-permute-start.30 = (bf16[2,2,2,2,32,3072]{5,4,3,2,1,0:T(8,128)(2,1)S(1)}, bf16[2,2,2,2,32,3072]{5,4,3,2,1,0:T(8,128)(2,1)}, u32[]{:S(2)}, u32[]{:S(2)}) collective-permute-start(bf16[2,2,2,2,32,3072]{5,4,3,2,1,0:T(8,128)(2,1)S(1)} %pad_maximum_fusion.7), channel_id=1, source_target_pairs={{0,2},{2,0},{4,6},{6,4},{8,10},{10,8},{12,14},{14,12},{16,18},{18,... | collective-permute-start | bytes 9437192 | tf_op jit(solution)/shard_map/ppermute | solution.py:94
  361.2 36.6 %collective-permute-start.63 = (bf16[2,2,2,96,1024]{4,3,2,1,0:T(8,128)(2,1)S(1)}, bf16[2,2,2,96,1024]{4,3,2,1,0:T(8,128)(2,1)}, u32[]{:S(2)}, u32[]{:S(2)}) collective-permute-start(bf16[2,2,2,96,1024]{4,3,2,1,0:T(8,128)(2,1)S(1)} %fusion.75), channel_id=1, source_target_pairs={{0,1},{1,0},{2,3},{3,2},{4,5},{5,4},{6,7},{7,6},{8,9},{9,8},{10,11... | collective-permute-start | bytes 4718600 | tf_op jit(solution)/shard_map/ppermute | solution.py:94
  402.5 18.8 %collective-permute-start.64 = (bf16[2,2,96,1024]{3,2,1,0:T(8,128)(2,1)S(1)}, bf16[2,2,96,1024]{3,2,1,0:T(8,128)(2,1)S(1)}, u32[]{:S(2)}, u32[]{:S(2)}) collective-permute-start(bf16[2,2,96,1024]{3,2,1,0:T(8,128)(2,1)S(1)} %fusion.99), channel_id=1, source_target_pairs={{0,4},{2,6},{4,0},{6,2},{8,12},{10,14},{12,8},{14,10},{16,20},{18,... | collective-permute-start | bytes 2359304 | tf_op jit(solution)/shard_map/ppermute | solution.py:94
  455.1 11.1 %collective-permute-start.32 = (bf16[2,96,1024]{2,1,0:T(8,128)(2,1)S(1)}, bf16[2,96,1024]{2,1,0:T(8,128)(2,1)S(1)}, u32[]{:S(2)}, u32[]{:S(2)}) collective-permute-start(bf16[2,96,1024]{2,1,0:T(8,128)(2,1)S(1)} %pad_maximum_fusion.32), channel_id=1, source_target_pairs={{0,8},{2,10},{4,12},{6,14},{8,0},{10,2},{12,4},{14,6},{16,24},{18,... | collective-permute-start | bytes 1179656 | tf_op jit(solution)/shard_map/ppermute | solution.py:94
  466.3 18.7 %collective-permute-start.33 = (bf16[2,2,96,1024]{3,2,1,0:T(8,128)(2,1)S(1)}, bf16[2,2,96,1024]{3,2,1,0:T(8,128)(2,1)S(1)}, u32[]{:S(2)}, u32[]{:S(2)}) collective-permute-start(bf16[2,2,96,1024]{3,2,1,0:T(8,128)(2,1)S(1)} %pad_maximum_fusion.24), channel_id=1, source_target_pairs={{0,1},{1,0},{2,3},{3,2},{4,5},{5,4},{6,7},{7,6},{8,9},{9,8},{10,11... | collective-permute-start | bytes 2359304 | tf_op jit(solution)/shard_map/ppermute | solution.py:94
  485.3 34.6 %collective-permute-start.34 = (bf16[2,2,2,96,1024]{4,3,2,1,0:T(8,128)(2,1)S(1)}, bf16[2,2,2,96,1024]{4,3,2,1,0:T(8,128)(2,1)S(1)}, u32[]{:S(2)}, u32[]{:S(2)}) collective-permute-start(bf16[2,2,2,96,1024]{4,3,2,1,0:T(8,128)(2,1)S(1)} %pad_maximum_fusion.16), channel_id=1, source_target_pairs={{0,4},{2,6},{4,0},{6,2},{8,12},{10,14},{12,8},{14,10},{16,20},{18,... | collective-permute-start | bytes 4718600 | tf_op jit(solution)/shard_map/ppermute | solution.py:94
  706.9 48.0 %collective-permute-start.36 = (bf16[1,2,1,512,1024]{4,3,2,1,0:T(8,128)(2,1)}, bf16[1,2,1,512,1024]{4,3,2,1,0:T(8,128)(2,1)}, u32[]{:S(2)}, u32[]{:S(2)}) collective-permute-start(bf16[1,2,1,512,1024]{4,3,2,1,0:T(8,128)(2,1)} %fusion.63), channel_id=1, source_target_pairs={{0,1},{1,0},{2,3},{3,2},{4,5},{5,4},{6,7},{7,6},{8,9},{9,8},{10,11... | collective-permute-start | bytes 6291464 | tf_op jit(solution)/shard_map/ppermute | solution.py:94
  721.8 79.5 %collective-permute-start.47 = (bf16[2,2,2,2,64,1024]{5,4,3,2,1,0:T(8,128)(2,1)}, bf16[2,2,2,2,64,1024]{5,4,3,2,1,0:T(8,128)(2,1)}, u32[]{:S(2)}, u32[]{:S(2)}) collective-permute-start(bf16[2,2,2,2,64,1024]{5,4,3,2,1,0:T(8,128)(2,1)} %fusion.61), channel_id=1, source_target_pairs={{0,2},{2,0},{4,6},{6,4},{8,10},{10,8},{12,14},{14,12},{16,18},{18,... | collective-permute-start | bytes 6291464 | tf_op jit(solution)/shard_map/ppermute | solution.py:94
  726.7 107.4 %collective-permute-start.57 = (bf16[2,2,2,2,32,3072]{5,4,0,1,2,3:T(8,128)(2,1)}, bf16[2,2,2,2,32,3072]{5,4,0,1,2,3:T(8,128)(2,1)}, u32[]{:S(2)}, u32[]{:S(2)}) collective-permute-start(bf16[2,2,2,2,32,3072]{5,4,0,1,2,3:T(8,128)(2,1)} %fusion.30), channel_id=1, source_target_pairs={{0,2},{2,0},{4,6},{6,4},{8,10},{10,8},{12,14},{14,12},{16,18},{18,... | collective-permute-start | bytes 9437192 | tf_op jit(solution)/shard_map/ppermute | solution.py:94
  732.1 117.3 %collective-permute-start.52 = (bf16[2,2,2,2,32,3072]{5,4,0,1,3,2:T(8,128)(2,1)}, bf16[2,2,2,2,32,3072]{5,4,0,1,3,2:T(8,128)(2,1)}, u32[]{:S(2)}, u32[]{:S(2)}) collective-permute-start(bf16[2,2,2,2,32,3072]{5,4,0,1,3,2:T(8,128)(2,1)} %fusion.29), channel_id=1, source_target_pairs={{0,2},{2,0},{4,6},{6,4},{8,10},{10,8},{12,14},{14,12},{16,18},{18,... | collective-permute-start | bytes 9437192 | tf_op jit(solution)/shard_map/ppermute | solution.py:94
  796.5 69.0 %collective-permute-start.42 = (bf16[2,2,2,2,32,2048]{5,4,0,1,3,2:T(8,128)(2,1)}, bf16[2,2,2,2,32,2048]{5,4,0,1,3,2:T(8,128)(2,1)}, u32[]{:S(2)}, u32[]{:S(2)}) collective-permute-start(bf16[2,2,2,2,32,2048]{5,4,0,1,3,2:T(8,128)(2,1)} %fusion.62), channel_id=1, source_target_pairs={{0,2},{2,0},{4,6},{6,4},{8,10},{10,8},{12,14},{14,12},{16,18},{18,... | collective-permute-start | bytes 6291464 | tf_op jit(solution)/shard_map/ppermute | solution.py:94
  806.8 24.3 %collective-permute-start.48 = (bf16[2,2,2,64,1024]{4,3,2,1,0:T(8,128)(2,1)S(1)}, bf16[2,2,2,64,1024]{4,3,2,1,0:T(8,128)(2,1)S(1)}, u32[]{:S(2)}, u32[]{:S(2)}) collective-permute-start(bf16[2,2,2,64,1024]{4,3,2,1,0:T(8,128)(2,1)S(1)} %fusion.81), channel_id=1, source_target_pairs={{0,4},{2,6},{4,0},{6,2},{8,12},{10,14},{12,8},{14,10},{16,20},{18,... | collective-permute-start | bytes 3145736 | tf_op jit(solution)/shard_map/ppermute | solution.py:94
  813.8 56.8 %collective-permute-start.37 = (bf16[2,2,2,2,32,2048]{5,4,3,2,1,0:T(8,128)(2,1)}, bf16[2,2,2,2,32,2048]{5,4,3,2,1,0:T(8,128)(2,1)}, u32[]{:S(2)}, u32[]{:S(2)}) collective-permute-start(bf16[2,2,2,2,32,2048]{5,4,3,2,1,0:T(8,128)(2,1)} %fusion.60), channel_id=1, source_target_pairs={{0,2},{2,0},{4,6},{6,4},{8,10},{10,8},{12,14},{14,12},{16,18},{18,... | collective-permute-start | bytes 6291464 | tf_op jit(solution)/shard_map/ppermute | solution.py:94
  833.0 14.9 %collective-permute-start.49 = (bf16[2,2,64,1024]{3,2,1,0:T(8,128)(2,1)S(1)}, bf16[2,2,64,1024]{3,2,1,0:T(8,128)(2,1)S(1)}, u32[]{:S(2)}, u32[]{:S(2)}) collective-permute-start(bf16[2,2,64,1024]{3,2,1,0:T(8,128)(2,1)S(1)} %fusion.103), channel_id=1, source_target_pairs={{0,1},{1,0},{2,3},{3,2},{4,5},{5,4},{6,7},{7,6},{8,9},{9,8},{10,11... | collective-permute-start | bytes 1572872 | tf_op jit(solution)/shard_map/ppermute | solution.py:94
  840.5 41.2 %collective-permute-start.58 = (bf16[2,2,2,32,3072]{4,3,0,1,2:T(8,128)(2,1)}, bf16[2,2,2,32,3072]{4,3,0,1,2:T(8,128)(2,1)}, u32[]{:S(2)}, u32[]{:S(2)}) collective-permute-start(bf16[2,2,2,32,3072]{4,3,0,1,2:T(8,128)(2,1)} %fusion.74), channel_id=1, source_target_pairs={{0,1},{1,0},{2,3},{3,2},{4,5},{5,4},{6,7},{7,6},{8,9},{9,8},{10,11... | collective-permute-start | bytes 4718600 | tf_op jit(solution)/shard_map/ppermute | solution.py:94
  858.3 37.4 %collective-permute-start.53 = (bf16[2,2,2,32,3072]{4,3,0,1,2:T(8,128)(2,1)S(1)}, bf16[2,2,2,32,3072]{4,3,0,1,2:T(8,128)(2,1)S(1)}, u32[]{:S(2)}, u32[]{:S(2)}) collective-permute-start(bf16[2,2,2,32,3072]{4,3,0,1,2:T(8,128)(2,1)S(1)} %fusion.73), channel_id=1, source_target_pairs={{0,4},{2,6},{4,0},{6,2},{8,12},{10,14},{12,8},{14,10},{16,20},{18,... | collective-permute-start | bytes 4718600 | tf_op jit(solution)/shard_map/ppermute | solution.py:94
  869.3 48.8 %collective-permute-start.43 = (bf16[2,2,2,32,2048]{4,3,0,1,2:T(8,128)(2,1)S(1)}, bf16[2,2,2,32,2048]{4,3,0,1,2:T(8,128)(2,1)S(1)}, u32[]{:S(2)}, u32[]{:S(2)}) collective-permute-start(bf16[2,2,2,32,2048]{4,3,0,1,2:T(8,128)(2,1)S(1)} %fusion.80), channel_id=1, source_target_pairs={{0,4},{2,6},{4,0},{6,2},{8,12},{10,14},{12,8},{14,10},{16,20},{18,... | collective-permute-start | bytes 3145736 | tf_op jit(solution)/shard_map/ppermute | solution.py:94
  873.1 46.5 %collective-permute-start.38 = (bf16[2,2,2,32,2048]{4,3,2,1,0:T(8,128)(2,1)S(1)}, bf16[2,2,2,32,2048]{4,3,2,1,0:T(8,128)(2,1)S(1)}, u32[]{:S(2)}, u32[]{:S(2)}) collective-permute-start(bf16[2,2,2,32,2048]{4,3,2,1,0:T(8,128)(2,1)S(1)} %fusion.79), channel_id=1, source_target_pairs={{0,1},{1,0},{2,3},{3,2},{4,5},{5,4},{6,7},{7,6},{8,9},{9,8},{10,11... | collective-permute-start | bytes 3145736 | tf_op jit(solution)/shard_map/ppermute | solution.py:94
  883.6 48.6 %collective-permute-start.59 = (bf16[2,2,32,3072]{3,2,0,1:T(8,128)(2,1)S(1)}, bf16[2,2,32,3072]{3,2,0,1:T(8,128)(2,1)S(1)}, u32[]{:S(2)}, u32[]{:S(2)}) collective-permute-start(bf16[2,2,32,3072]{3,2,0,1:T(8,128)(2,1)S(1)} %fusion.98), channel_id=1, source_target_pairs={{0,4},{2,6},{4,0},{6,2},{8,12},{10,14},{12,8},{14,10},{16,20},{18,... | collective-permute-start | bytes 2359304 | tf_op jit(solution)/shard_map/ppermute | solution.py:94
  896.1 37.4 %collective-permute-start.54 = (bf16[2,2,32,3072]{3,2,0,1:T(8,128)(2,1)S(1)}, bf16[2,2,32,3072]{3,2,0,1:T(8,128)(2,1)S(1)}, u32[]{:S(2)}, u32[]{:S(2)}) collective-permute-start(bf16[2,2,32,3072]{3,2,0,1:T(8,128)(2,1)S(1)} %fusion.97), channel_id=1, source_target_pairs={{0,1},{1,0},{2,3},{3,2},{4,5},{5,4},{6,7},{7,6},{8,9},{9,8},{10,11... | collective-permute-start | bytes 2359304 | tf_op jit(solution)/shard_map/ppermute | solution.py:94
  918.5 16.4 %collective-permute-start.44 = (bf16[2,2,32,2048]{3,2,0,1:T(8,128)(2,1)S(1)}, bf16[2,2,32,2048]{3,2,0,1:T(8,128)(2,1)S(1)}, u32[]{:S(2)}, u32[]{:S(2)}) collective-permute-start(bf16[2,2,32,2048]{3,2,0,1:T(8,128)(2,1)S(1)} %fusion.102), channel_id=1, source_target_pairs={{0,1},{1,0},{2,3},{3,2},{4,5},{5,4},{6,7},{7,6},{8,9},{9,8},{10,11... | collective-permute-start | bytes 1572872 | tf_op jit(solution)/shard_map/ppermute | solution.py:94
  920.0 17.9 %collective-permute-start.39 = (bf16[2,2,32,2048]{3,2,1,0:T(8,128)(2,1)S(1)}, bf16[2,2,32,2048]{3,2,1,0:T(8,128)(2,1)S(1)}, u32[]{:S(2)}, u32[]{:S(2)}) collective-permute-start(bf16[2,2,32,2048]{3,2,1,0:T(8,128)(2,1)S(1)} %fusion.101), channel_id=1, source_target_pairs={{0,4},{2,6},{4,0},{6,2},{8,12},{10,14},{12,8},{14,10},{16,20},{18,... | collective-permute-start | bytes 1572872 | tf_op jit(solution)/shard_map/ppermute | solution.py:94
  932.5 13.1 %collective-permute-start.60 = (bf16[2,32,3072]{2,1,0:T(8,128)(2,1)S(1)}, bf16[2,32,3072]{2,1,0:T(8,128)(2,1)S(1)}, u32[]{:S(2)}, u32[]{:S(2)}) collective-permute-start(bf16[2,32,3072]{2,1,0:T(8,128)(2,1)S(1)} %fusion.108), channel_id=1, source_target_pairs={{0,8},{2,10},{4,12},{6,14},{8,0},{10,2},{12,4},{14,6},{16,24},{18,... | collective-permute-start | bytes 1179656 | tf_op jit(solution)/shard_map/ppermute | solution.py:94
  933.8 19.6 %collective-permute-start.55 = (bf16[2,32,3072]{2,1,0:T(8,128)(2,1)S(1)}, bf16[2,32,3072]{2,1,0:T(8,128)(2,1)S(1)}, u32[]{:S(2)}, u32[]{:S(2)}) collective-permute-start(bf16[2,32,3072]{2,1,0:T(8,128)(2,1)S(1)} %fusion.107), channel_id=1, source_target_pairs={{0,8},{2,10},{4,12},{6,14},{8,0},{10,2},{12,4},{14,6},{16,24},{18,... | collective-permute-start | bytes 1179656 | tf_op jit(solution)/shard_map/ppermute | solution.py:94
  935.1 21.1 %collective-permute-start.45 = (bf16[2,32,2048]{2,1,0:T(8,128)(2,1)S(1)}, bf16[2,32,2048]{2,1,0:T(8,128)(2,1)S(1)}, u32[]{:S(2)}, u32[]{:S(2)}) collective-permute-start(bf16[2,32,2048]{2,1,0:T(8,128)(2,1)S(1)} %fusion.114), channel_id=1, source_target_pairs={{0,8},{2,10},{4,12},{6,14},{8,0},{10,2},{12,4},{14,6},{16,24},{18,... | collective-permute-start | bytes 786440 | tf_op jit(solution)/shard_map/ppermute | solution.py:94
  938.1 21.0 %collective-permute-start.40 = (bf16[2,32,2048]{2,1,0:T(8,128)(2,1)S(1)}, bf16[2,32,2048]{2,1,0:T(8,128)(2,1)S(1)}, u32[]{:S(2)}, u32[]{:S(2)}) collective-permute-start(bf16[2,32,2048]{2,1,0:T(8,128)(2,1)S(1)} %fusion.113), channel_id=1, source_target_pairs={{0,8},{2,10},{4,12},{6,14},{8,0},{10,2},{12,4},{14,6},{16,24},{18,... | collective-permute-start | bytes 786440 | tf_op jit(solution)/shard_map/ppermute | solution.py:94
  945.7 13.7 %collective-permute-start.61 = (bf16[32,3072]{1,0:T(8,128)(2,1)S(1)}, bf16[32,3072]{1,0:T(8,128)(2,1)S(1)}, u32[]{:S(2)}, u32[]{:S(2)}) collective-permute-start(bf16[32,3072]{1,0:T(8,128)(2,1)S(1)} %fusion.117), channel_id=1, source_target_pairs={{0,16},{2,18},{4,20},{6,22},{8,24},{10,26},{12,28},{14,30},{16,0},... | collective-permute-start | bytes 589832 | tf_op jit(solution)/shard_map/ppermute | solution.py:94
  953.5 13.5 %collective-permute-start.56 = (bf16[32,3072]{1,0:T(8,128)(2,1)S(1)}, bf16[32,3072]{1,0:T(8,128)(2,1)S(1)}, u32[]{:S(2)}, u32[]{:S(2)}) collective-permute-start(bf16[32,3072]{1,0:T(8,128)(2,1)S(1)} %fusion.116), channel_id=1, source_target_pairs={{0,16},{2,18},{4,20},{6,22},{8,24},{10,26},{12,28},{14,30},{16,0},... | collective-permute-start | bytes 589832 | tf_op jit(solution)/shard_map/ppermute | solution.py:94
  956.2 12.7 %collective-permute-start.46 = (bf16[32,2048]{1,0:T(8,128)(2,1)S(1)}, bf16[32,2048]{1,0:T(8,128)(2,1)S(1)}, u32[]{:S(2)}, u32[]{:S(2)}) collective-permute-start(bf16[32,2048]{1,0:T(8,128)(2,1)S(1)} %fusion.120), channel_id=1, source_target_pairs={{0,16},{2,18},{4,20},{6,22},{8,24},{10,26},{12,28},{14,30},{16,0},... | collective-permute-start | bytes 393224 | tf_op jit(solution)/shard_map/ppermute | solution.py:94
  (143 other events, 2322.7 us)
